TPU v7x, 128 devices: a whole 4x4x4 slice. The times are simulated.
128 devices in a mesh: shard: 128 (over x, z, y, core).
Axes of the slice: x: 4, y: 4, z: 4, core: 2. Of those that a mesh axis runs over, the one named last changes fastest.
Arguments:
- queries: bfloat16 [32768, 256], P('shard')
- clusters: int32 [32768, 8], P('shard'), may hold values from 0 to 2047, all different within a row; in each aligned block of 256 rows (0 to 255, 256 to 511, ...) at most 2 rows name the same one
- placement: int32 [2048], replicated, may hold values from 0 to 2047, each once
- pos_pick: int32 [32768], P('shard'), may hold values from 0 to 7
- pos_row: int32 [32768], P('shard'), may hold values from 0 to 255
- counts: int32 [2048], P('shard'), may hold values from 1 to 256, as said below
- labels: bfloat16 [2048, 256, 256], P('shard'), may hold values from -6 to 6
- accum: float32 [2048, 256], P('shard'), may hold values from 0.01 to 1
Outputs:
- new_labels: float32 [2048, 256, 256], P('shard')
- new_accum: float32 [2048, 256], P('shard')
- query_grad: bfloat16 [32768, 256], P('shard')
- loss: float32 [32768], P('shard')
Inputs may be any that keep to these rules, and one draw needn't show every extreme that they name: A query's 8 clusters are distinct; among the queries of one device no cluster is named more than 2 times, a bound that some block reaches. `counts`: some block has all 256 rows valid.
All inputs are finite; a program needn't handle non-finite values.
Results may differ from a plain program's by a relative error of at most 0.0031.
Values may be sent and summed in bfloat16 or wider, within the bound.
No kernel may reach another device: no remote copies, remote signals or barrier semaphores. Data moves between devices by JAX's collectives and lax.ppermute only.
A program may use at most 64 MiB of HBM per device.

v0:
```python
import jax
import jax.numpy as jnp
from jax import lax
from jax.experimental import pallas as pl
from jax.experimental.pallas import tpu as pltpu
from jax.sharding import PartitionSpec as P

STEP_RATE = 0.1
DEVS = 128
GROUP = 8
SLOTS = 32
CHUNK = 72
BLOCK = GROUP * CHUNK
NGROUPS = DEVS // GROUP
f32 = jnp.float32
bf16 = jnp.bfloat16
i32 = jnp.int32


def iota(shape, dim):
    return lax.broadcasted_iota(i32, shape, dim)


def one(mask):
    return jnp.where(mask, 1.0, 0.0).astype(bf16)


def dot(a, b, ca=1, cb=0):
    return lax.dot_general(a, b, (((ca,), (cb,)), ((), ())), preferred_element_type=f32)


def pieces_of(x):
    hi = x.astype(bf16).astype(f32)
    rest = x - hi
    mid = rest.astype(bf16).astype(f32)
    return hi, mid, rest - mid


def total(x):
    return jnp.sum(x, axis=0, keepdims=True)


def to_rows(rows, extra):
    left = rows[:, :128].reshape(GROUP, SLOTS, 128)
    right = rows[:, 128:].reshape(GROUP, SLOTS, 128)
    return jnp.concatenate([left, right, extra], axis=1).reshape(BLOCK, 128).astype(bf16)


def from_rows(ref, group):
    block = ref[pl.ds(pl.multiple_of(group * BLOCK, BLOCK), BLOCK), :]
    return block.astype(f32).reshape(GROUP, CHUNK, 128)


def slot_rows(block):
    left = block[:, :SLOTS].reshape(GROUP * SLOTS, 128)
    right = block[:, SLOTS : 2 * SLOTS].reshape(GROUP * SLOTS, 128)
    return jnp.concatenate([left, right], axis=1).astype(bf16)


def route_kernel(cl_ref, place_ref, pick_ref, row_ref, q_ref, send_ref, sid_ref, ext_scr):
    c = cl_ref[...]
    ch, cl = c >> 7, c & 127
    place = place_ref[...]
    table = jnp.concatenate([(place >> 4).astype(f32), (place & 15).astype(f32)], axis=0).astype(bf16)
    i128, i16, i32s = iota((128, 256), 0), iota((16, 256), 0), iota((32, 256), 0)
    query = iota((1, 256), 1)
    queryf = query.astype(f32)
    ds, ls, ohs = [], [], []
    acc = jnp.zeros((32, 128), f32)
    for k in range(8):
        got = dot(table, one(i128 == cl[k : k + 1]))
        mine = i16 == ch[k : k + 1]
        d = total(jnp.where(mine, got[:16], 0.0)).astype(i32)
        l = total(jnp.where(mine, got[16:], 0.0)).astype(i32)
        oh = one(i128 == d)
        is_l = i16 == l
        named = jnp.concatenate([jnp.where(is_l, 1.0, 0.0), jnp.where(is_l, queryf, 0.0)], axis=0)
        acc = acc + dot(named.astype(bf16), oh, 1, 1)
        ds.append(d)
        ls.append(l)
        ohs.append(oh)
    count = acc[:16]
    middle = jnp.where(count > 1.5, jnp.floor(acc[16:] * 0.5), 255.0).astype(bf16)
    rls, sids = [], []
    for k in range(8):
        got = dot(middle, ohs[k])
        border = total(jnp.where(i16 == ls[k], got, 0.0)).astype(i32)
        rl = jnp.where(query > border, 16, 0) + ls[k]
        rls.append(rl)
        sids.append(ds[k] * SLOTS + rl)
    pick = pick_ref[...]
    dp = jnp.zeros((1, 256), i32)
    rlp = jnp.zeros((1, 256), i32)
    for k in range(8):
        dp = jnp.where(pick == k, ds[k], dp)
        rlp = jnp.where(pick == k, rls[k], rlp)
    ohp = one(i128 == dp)
    before = one(iota((256, 256), 0) < iota((256, 256), 1))
    j = total(ohp.astype(f32) * dot(ohp, before)).astype(i32)
    w_t = jnp.where(i32s == rlp, (row_ref[...] + 1).astype(f32), 0.0)
    w_j = jnp.where(i32s == j, (rlp + 1).astype(f32), 0.0)
    res = dot(jnp.concatenate([w_t, w_j, jnp.ones((8, 256), f32)], axis=0).astype(bf16), ohp, 1, 1)
    want = res[64:65]
    free = jnp.where(jnp.concatenate([count, count - 1.0], axis=0) < 0.5, 1.0, 0.0)
    lower = one(iota((32, 32), 1) < iota((32, 32), 0))
    turn = dot(lower, free.astype(bf16))
    turn = jnp.where(free > 0.5, turn, 99.0)
    code = jnp.zeros((32, 128), f32)
    for s in range(SLOTS):
        code = jnp.where(turn == float(s), res[32 + s : 33 + s], code)
    short = jnp.max(jnp.where(want > total(free), 1.0, 0.0), axis=1, keepdims=True)
    got = dot(turn.astype(bf16), ohp)
    carrier = total(jnp.where(got == j.astype(f32), i32s.astype(f32), 0.0)).astype(i32)
    ext = jnp.concatenate([res[:32], code, jnp.broadcast_to(short, (64, 128))], axis=0)
    ext_scr[...] = ext.T
    sid_ref[...] = jnp.concatenate(
        sids + [dp * SLOTS + carrier, dp * SLOTS + rlp] + [jnp.zeros((1, 256), i32)] * 6, axis=0
    )

    def group(g, _):
        slot = iota((256, 256), 0) + g * 256
        mask = slot == sid_ref[0:1, :]
        for k in range(1, 8):
            mask = mask | (slot == sid_ref[k : k + 1, :])
        rows = dot(one(mask), q_ref[...])
        extra = ext_scr[pl.ds(pl.multiple_of(g * GROUP, GROUP), GROUP), :]
        extra = jnp.broadcast_to(extra[:, None, :], (GROUP, 8, 128))
        send_ref[pl.ds(pl.multiple_of(g * BLOCK, BLOCK), BLOCK), :] = to_rows(rows, extra)
        return 0

    lax.fori_loop(0, NGROUPS, group, 0, unroll=2)


def by_slot(x):
    second = pltpu.roll(x, 112, 1)
    both = jnp.concatenate(
        [x.reshape(NGROUPS, 1, GROUP, 128), second.reshape(NGROUPS, 1, GROUP, 128)], axis=1
    )
    return both.reshape(256, 128).T


def owner_kernel(
    counts_ref, cc_ref, recv_ref, lab_ref, x_ref, tr_ref, flag_ref, send_ref,
    ext_scr, part_scr, pos_scr, stat_scr, back_scr,
):
    r256, c256 = iota((256, 256), 0), iota((256, 256), 1)
    sent = (r256 & 7) * 32 + ((r256 >> 3) & 1) * 16 + (r256 >> 4)
    perm = one(c256 == sent)

    def gather(g, _):
        block = from_rows(recv_ref, g)
        x = dot(perm, slot_rows(block)).astype(bf16)
        for l in range(16):
            x_ref[l, pl.ds(pl.multiple_of(g * 16, 16), 16), :] = x[l * 16 : (l + 1) * 16]
        ext_scr[pl.ds(pl.multiple_of(g * 64, 64), 64), :] = block[:, 64:72].reshape(64, 128)
        return 0

    lax.fori_loop(0, NGROUPS, gather, 0, unroll=2)
    ext = ext_scr[pl.ds(0, 128, stride=8), :]
    slots = by_slot(ext)
    flag_ref[...] = jnp.broadcast_to(jnp.max(slots[64:65], axis=1, keepdims=True), (8, 128))
    raw = slots[:16] - 1.0
    cc = cc_ref[...]
    tr_ref[...] = jnp.where(raw > -0.5, raw - cc * jnp.floor((raw + 0.5) / cc), -1.0)
    stat_scr[...] = jnp.zeros((64, 256), f32)

    def cluster(l, _):
        lab = lab_ref[l]
        score = dot(lab, x_ref[l], 1, 1)
        masked = jnp.where(r256 < counts_ref[l], score, -jnp.inf)
        top = jnp.max(masked, axis=0, keepdims=True)
        weight = jnp.exp(masked - top)
        hit = r256.astype(f32) == tr_ref[pl.ds(l, 1), :]
        stat_scr[pl.ds(l, 1), :] = top
        stat_scr[pl.ds(l + 16, 1), :] = total(weight)
        stat_scr[pl.ds(l + 32, 1), :] = total(jnp.where(hit, score, 0.0))
        part_scr[l] = dot(weight.astype(bf16), lab, 0, 0).astype(bf16)
        pos_scr[l] = dot(one(hit), lab, 0, 0).astype(bf16)
        return 0

    lax.fori_loop(0, 16, cluster, 0, unroll=2)
    hi, mid, lo = pieces_of(stat_scr[...])
    first = jnp.concatenate([hi, mid], axis=0).T.reshape(NGROUPS, 2, GROUP, 128)
    second = jnp.concatenate([lo, jnp.zeros((64, 256), f32)], axis=0).T.reshape(NGROUPS, 2, GROUP, 128)
    back_scr[...] = jnp.zeros((1024, 128), f32)
    for r in range(2):
        back_scr[pl.ds(2 * r, 128, stride=8), :] = first[:, r].reshape(128, 128)
        back_scr[pl.ds(2 * r + 1, 128, stride=8), :] = second[:, r].reshape(128, 128)

    back = (c256 & 7) * 32 + ((c256 >> 3) & 1) * 16 + (c256 >> 4)
    unperm = one(r256 == back)
    wanted = jnp.where((r256 >> 5) == (c256 & 7), (back & 31) + 1, -1).astype(f32)
    own_lane = iota((256, 128), 1) == 32 + (iota((256, 128), 0) & 31)
    ones = jnp.ones((128, 256), bf16)

    def scatter(g, _):
        at = pl.ds(pl.multiple_of(g * 16, 16), 16)
        parts = jnp.concatenate([part_scr[l, at, :] for l in range(16)], axis=0)
        pos = jnp.concatenate([pos_scr[l, at, :] for l in range(16)], axis=0)
        codes = ext_scr[pl.ds(pl.multiple_of(g * 64, 64), 64), :].reshape(GROUP, 8, 128)
        codes = jnp.concatenate([codes] * 4, axis=1).reshape(256, 128)
        code = dot(jnp.where(own_lane, codes, 0.0).astype(bf16), ones)
        rows = jnp.where(code > 0.5, dot(one(code == wanted), pos), dot(unperm, parts))
        extra = back_scr[pl.ds(pl.multiple_of(g * 64, 64), 64), :].reshape(GROUP, 8, 128)
        send_ref[pl.ds(pl.multiple_of(g * BLOCK, BLOCK), BLOCK), :] = to_rows(rows, extra)
        return 0

    lax.fori_loop(0, NGROUPS, scatter, 0, unroll=2)


def lse_kernel(recv_ref, sid_ref, loss_ref, send_ref, scale_ref, ext_scr):
    def take(g, _):
        block = from_rows(recv_ref, g)
        ext_scr[pl.ds(pl.multiple_of(g * 64, 64), 64), :] = block[:, 64:72].reshape(64, 128)
        return 0

    lax.fori_loop(0, NGROUPS, take, 0, unroll=2)
    stats = []
    for r in range(2):
        first = ext_scr[pl.ds(2 * r, 128, stride=8), :]
        second = ext_scr[pl.ds(2 * r + 1, 128, stride=8), :]
        stats.append(first + pltpu.roll(first, 64, 1) + second)
    both = jnp.where(iota((128, 128), 1) < 64, stats[0], pltpu.roll(stats[1], 64, 1)).T
    table = jnp.concatenate(pieces_of(both), axis=0).astype(bf16)
    i128, i16, i32s = iota((128, 256), 0), iota((16, 256), 0), iota((32, 256), 0)
    sid = sid_ref[...]
    tops, sums, ohs = [], [], []
    target = jnp.zeros((1, 256), f32)
    for k in range(8):
        s = sid[k : k + 1]
        oh = one(i128 == (s >> 5))
        got = dot(table, oh)
        got = got[:128] + got[128:256] + got[256:]
        got = jnp.where((s & 16) == 0, got[:48], got[64:112])
        mine = i16 == (s & 15)
        tops.append(total(jnp.where(mine, got[:16], 0.0)))
        sums.append(total(jnp.where(mine, got[16:32], 0.0)))
        target = target + total(jnp.where(mine, got[32:48], 0.0))
        ohs.append(oh)
    largest = tops[0]
    for k in range(1, 8):
        largest = jnp.maximum(largest, tops[k])
    norm = sums[0] * jnp.exp(tops[0] - largest)
    for k in range(1, 8):
        norm = norm + sums[k] * jnp.exp(tops[k] - largest)
    lse = largest + jnp.log(norm)
    loss_ref[...] = lse - target
    scale_ref[...] = jnp.concatenate([jnp.exp(t - lse) for t in tops], axis=0)
    split = pieces_of(lse)
    out = jnp.zeros((96, 128), f32)
    for k in range(8):
        mine = i32s == (sid[k : k + 1] & 31)
        w = jnp.concatenate([jnp.where(mine, p, 0.0) for p in split], axis=0)
        out = out + dot(w.astype(bf16), ohs[k], 1, 1)
    out = out[:32] + out[32:64] + out[64:]
    send_ref[...] = jnp.concatenate([out, jnp.zeros((96, 128), f32)], axis=0).T


def combine_kernel(flag_ref, recv_ref, sid_ref, scale_ref, out_ref):
    pos_weight = jnp.where(flag_ref[0:1, :] > 0.5, 0.0, -1.0)
    pos_weight = jnp.concatenate([pos_weight, pos_weight], axis=1)
    cols = jnp.concatenate(
        [sid_ref[...].astype(f32), scale_ref[...], pos_weight, jnp.zeros((103, 256), f32)], axis=0
    ).T
    lane = iota((256, 256), 1).astype(f32)

    def group(g, acc):
        rows = slot_rows(from_rows(recv_ref, g))
        slot = lane + (g * 256).astype(f32)
        a = jnp.where(cols[:, 8:9] == slot, cols[:, 24:25], 0.0)
        for k in range(8):
            a = jnp.where(cols[:, k : k + 1] == slot, cols[:, 16 + k : 17 + k], a)
        hi = a.astype(bf16)
        lo = (a - hi.astype(f32)).astype(bf16)
        return acc + (dot(hi, rows) + dot(lo, rows))

    out_ref[...] = lax.fori_loop(0, NGROUPS, group, jnp.zeros((256, 256), f32))


def table_kernel(counts_ref, lse_ref, tr_ref, acc_ref, x_ref, lab_ref, new_ref, nacc_ref, lse_scr, acc_scr, out_scr):
    l = pl.program_id(0)

    @pl.when(l == 0)
    def _():
        lse_scr[...] = by_slot(lse_ref[...])
        acc_scr[...] = jnp.concatenate([acc_ref[...], jnp.zeros((112, 256), f32)], axis=0).T
        out_scr[...] = jnp.zeros((256, 128), f32)

    r256 = iota((256, 256), 0)
    x, lab = x_ref[0], lab_ref[0]
    score = dot(lab, x, 1, 1)
    prob = jnp.where(r256 < counts_ref[l], jnp.exp(score - lse_scr[pl.ds(l, 1), :]), 0.0)
    hit = r256.astype(f32) == tr_ref[pl.ds(l, 1), :]
    dlogit = (prob - jnp.where(hit, 1.0, 0.0)).astype(bf16)
    grad = dot(dlogit, x)
    square = grad * grad
    mine = iota((256, 128), 1) == l
    both = (square[:, :128] + square[:, 128:]) * (1.0 / 256.0) + jnp.where(mine, acc_scr[...], 0.0)
    accum = jnp.sum(both, axis=1, keepdims=True)
    new_ref[0] = lab.astype(f32) - (STEP_RATE * grad) / jnp.sqrt(accum)
    out_scr[...] = jnp.where(mine, accum, out_scr[...])

    @pl.when(l == 15)
    def _():
        nacc_ref[...] = out_scr[...].T[:16]


def params(mib=40):
    return pltpu.CompilerParams(vmem_limit_bytes=mib * 1024 * 1024)


def shape(*dims, dtype=f32):
    return jax.ShapeDtypeStruct(dims, dtype)


VMEM = pl.BlockSpec(memory_space=pltpu.VMEM)
SMEM = pl.BlockSpec(memory_space=pltpu.SMEM)


def exchange(x):
    return lax.all_to_all(x, "shard", split_axis=0, concat_axis=0, tiled=True)


def shards(queries, clusters, placement, pos_pick, pos_row, counts, labels, accum):
    rows = DEVS * CHUNK
    send, sid = pl.pallas_call(
        route_kernel,
        out_shape=(shape(rows, 128, dtype=bf16), shape(16, 256, dtype=i32)),
        in_specs=[VMEM] * 5,
        out_specs=(VMEM, VMEM),
        scratch_shapes=[pltpu.VMEM((128, 128), f32)],
        compiler_params=params(),
        name="route",
    )(clusters.T, placement.reshape(16, 128), pos_pick.reshape(1, 256), pos_row.reshape(1, 256), queries)
    recv = exchange(send)
    x, target, flag, send = pl.pallas_call(
        owner_kernel,
        out_shape=(
            shape(16, 256, 256, dtype=bf16), shape(16, 256), shape(8, 128), shape(rows, 128, dtype=bf16),
        ),
        in_specs=[SMEM, VMEM, VMEM, VMEM],
        out_specs=(VMEM,) * 4,
        scratch_shapes=[
            pltpu.VMEM((1024, 128), f32),
            pltpu.VMEM((16, 256, 256), bf16),
            pltpu.VMEM((16, 256, 256), bf16),
            pltpu.VMEM((64, 256), f32),
            pltpu.VMEM((1024, 128), f32),
        ],
        compiler_params=params(),
        name="owner",
    )(counts, counts.astype(f32).reshape(16, 1), recv, labels)
    recv = exchange(send)
    loss, send, scale = pl.pallas_call(
        lse_kernel,
        out_shape=(shape(1, 256), shape(DEVS, 128), shape(8, 256)),
        in_specs=[VMEM, VMEM],
        out_specs=(VMEM,) * 3,
        scratch_shapes=[pltpu.VMEM((1024, 128), f32)],
        compiler_params=params(),
        name="normalizer",
    )(recv, sid)
    lse = exchange(send)
    query_grad = pl.pallas_call(
        combine_kernel,
        out_shape=shape(256, 256),
        in_specs=[VMEM] * 4,
        out_specs=VMEM,
        compiler_params=params(),
        cost_estimate=pl.CostEstimate(flops=2 * 2 * 256 * 4096 * 256, bytes_accessed=3_000_000, transcendentals=0),
        name="combine",
    )(flag, recv, sid, scale)

    def with_rows(grad):
        hit = jnp.arange(256, dtype=f32)[None, None, :] == target[:, :, None]
        found = jnp.einsum("csl,clw->csw", hit.astype(bf16), labels, preferred_element_type=f32).astype(bf16)
        found = found.reshape(16, NGROUPS, 2, GROUP, 256).transpose(1, 3, 2, 0, 4).reshape(DEVS * SLOTS, 256)
        return grad - exchange(found)[sid[9]].astype(f32)

    query_grad = lax.cond(flag[0, 0] > 0.5, with_rows, lambda grad: grad, query_grad).astype(bf16)
    whole = lambda *dims: pl.BlockSpec(dims, lambda l: (0,) * len(dims))
    per = pl.BlockSpec((1, 256, 256), lambda l: (l, 0, 0))
    new_labels, new_accum = pl.pallas_call(
        table_kernel,
        grid=(16,),
        out_shape=(shape(16, 256, 256), shape(16, 256)),
        in_specs=[SMEM, whole(128, 128), whole(16, 256), whole(16, 256), per, per],
        out_specs=(per, whole(16, 256)),
        scratch_shapes=[pltpu.VMEM((128, 256), f32), pltpu.VMEM((256, 128), f32), pltpu.VMEM((256, 128), f32)],
        compiler_params=params(),
        name="table",
    )(counts, lse, target, accum, x, labels)
    return (new_labels, new_accum, query_grad, loss.reshape(256))


def solution(mesh):
    return jax.shard_map(
        shards,
        mesh=mesh,
        in_specs=(
            P("shard", None), P("shard", None), P(), P("shard"), P("shard"), P("shard"),
            P("shard", None, None), P("shard", None),
        ),
        out_specs=(P("shard", None, None), P("shard", None), P("shard", None), P("shard")),
        check_vma=False,
    )
```

profile of v0, /device:TPU:1, one launch (start us, length us, event | category | flops | bytes accessed | tf_op | source)
XLA Modules:
  0.0 155.3 jit_solution(17542507534818804181)
XLA Ops:
  0.6 0.0 copy-start.4
  0.6 0.9 copy-done.4
  1.5 0.0 copy-start.6
  1.5 0.7 copy-done.6
  2.2 0.0 copy-start.7
  2.2 0.7 copy-done.7
  2.9 0.0 copy-start.9
  2.9 0.7 copy-done.9
  3.6 0.0 copy-start.10
  3.6 0.7 copy-done.10
  4.3 6.0 %route.1 = (bf16[9216,128]{1,0:T(8,128)(2,1)S(1)}, s32[16,256]{1,0:T(8,128)S(1)}) custom-call(s32[8,256]{1,0:T(8,128)S(1)} %bitcast.31, s32[16,128]{1,0:T(8,128)S(1)} %bitcast.32, s32[1,256]{1,0:T(1,128)S(1)} %bitcast.33, s32[1,256]{1,0:T(1,128)S(1)} %bitcast.34, bf16[256,256]{1,0:T(8,128)(2,1)S(1)} %copy-done.4), custom_call_target="tpu_custom_call" | custom-call | tf_op jit(solution)/shard_map/route/pallas_call | solution.py:326
  10.3 0.0 copy-start.1
  10.3 1.4 copy-done.1
  11.7 0.0 copy-start.8
  11.7 11.5 %all-to-all-start.1 = ((bf16[128,72,128]{2,1,0:T(8,128)(2,1)}), bf16[128,72,128]{2,1,0:T(8,128)(2,1)S(1)}, u32[]{:S(2)}, u32[]{:S(2)}) async-start(bf16[128,72,128]{2,1,0:T(8,128)(2,1)} %bitcast.29), calls=%async_computation.1 | async-start | bytes 4718592 | tf_op jit(solution)/shard_map/all_to_all | solution.py:321
  23.2 0.0 copy-done.8
  23.2 0.1 copy.16.cc_ref
  23.3 33.2 %all-to-all-done.1 = bf16[128,72,128]{2,1,0:T(8,128)(2,1)S(1)} async-done(((bf16[128,72,128]{2,1,0:T(8,128)(2,1)}), bf16[128,72,128]{2,1,0:T(8,128)(2,1)S(1)}, u32[]{:S(2)}, u32[]{:S(2)}) %all-to-all-start.1) | async-done | bytes 2359328 | tf_op jit(solution)/shard_map/all_to_all | solution.py:321
  56.5 13.7 %owner.1 = (bf16[16,256,256]{2,1,0:T(8,128)(2,1)S(1)}, f32[16,256]{1,0:T(8,128)S(1)}, f32[8,128]{1,0:T(8,128)S(1)}, bf16[9216,128]{1,0:T(8,128)(2,1)S(1)}) custom-call(s32[16]{0:T(128)S(1)} %copy-done.8, f32[16,1]{1,0:T(8,128)S(1)} %copy.16.cc_ref, bf16[9216,128]{1,0:T(8,128)(2,1)S(1)} %bitcast.27, bf16[16,256,256]{2,1,0:T(8,128)(2,1)} %lab_ref.3), custom_call_target="tpu_custom_call" | custom-call | tf_op jit(solution)/shard_map/owner/pallas_call | solution.py:336
  70.2 0.0 copy-start
  70.2 1.4 copy-done
  71.6 0.0 copy-start.2
  71.6 1.3 copy-done.2
  72.9 4.5 %all-to-all-start.2 = ((bf16[128,72,128]{2,1,0:T(8,128)(2,1)}), bf16[128,72,128]{2,1,0:T(8,128)(2,1)S(1)}, u32[]{:S(2)}, u32[]{:S(2)}) async-start(bf16[128,72,128]{2,1,0:T(8,128)(2,1)} %bitcast.28), calls=%async_computation.2 | async-start | bytes 4718592 | tf_op jit(solution)/shard_map/all_to_all | solution.py:321
  77.4 0.5 slice.6
  78.6 32.2 %all-to-all-done.2 = bf16[128,72,128]{2,1,0:T(8,128)(2,1)S(1)} async-done(((bf16[128,72,128]{2,1,0:T(8,128)(2,1)}), bf16[128,72,128]{2,1,0:T(8,128)(2,1)S(1)}, u32[]{:S(2)}, u32[]{:S(2)}) %all-to-all-start.2) | async-done | bytes 2359328 | tf_op jit(solution)/shard_map/all_to_all | solution.py:321
  110.8 2.1 %normalizer.1 = (f32[1,256]{1,0:T(1,128)}, f32[128,128]{1,0:T(8,128)}, f32[8,256]{1,0:T(8,128)S(1)}) custom-call(bf16[9216,128]{1,0:T(8,128)(2,1)S(1)} %bitcast.25, s32[16,256]{1,0:T(8,128)S(1)} %get-tuple-element.39.sid_ref), custom_call_target="tpu_custom_call" | custom-call | tf_op jit(solution)/shard_map/normalizer/pallas_call | solution.py:354
  112.9 14.5 %combine.1 = f32[256,256]{1,0:T(8,128)S(1)} custom-call(f32[8,128]{1,0:T(8,128)S(1)} %get-tuple-element.45.flag_ref, bf16[9216,128]{1,0:T(8,128)(2,1)S(1)} %bitcast.26, s32[16,256]{1,0:T(8,128)S(1)} %get-tuple-element.39.sid_ref, f32[8,256]{1,0:T(8,128)S(1)} %get-tuple-element.46.scale_ref), custom_call_target="tpu_custom_call" | custom-call | flops 1073741824 | bytes 3000000 | tf_op jit(solution)/shard_map/combine/pallas_call | solution.py:364
  127.4 0.0 copy-start.3
  127.4 0.0 copy-start.5
  127.4 4.6 %all-to-all-start.3 = ((f32[128,1,128]{2,1,0:T(1,128)}), f32[128,1,128]{2,1,0:T(1,128)S(1)}, u32[]{:S(2)}, u32[]{:S(2)}) async-start(f32[128,1,128]{2,1,0:T(1,128)} %bitcast.16), calls=%async_computation.3 | async-start | bytes 131072 | tf_op jit(solution)/shard_map/all_to_all | solution.py:321
  132.0 0.7 convert_element_type.28
  132.7 9.0 %all-to-all-done.3 = f32[128,1,128]{2,1,0:T(1,128)S(1)} async-done(((f32[128,1,128]{2,1,0:T(1,128)}), f32[128,1,128]{2,1,0:T(1,128)S(1)}, u32[]{:S(2)}, u32[]{:S(2)}) %all-to-all-start.3) | async-done | bytes 65568 | tf_op jit(solution)/shard_map/all_to_all | solution.py:321
  141.7 0.0 copy-done.3
  141.7 0.0 copy-done.5
  141.7 13.6 %table.1 = (f32[16,256,256]{2,1,0:T(8,128)}, f32[16,256]{1,0:T(8,128)}) custom-call(s32[16]{0:T(128)S(1)} %copy-done.8, f32[128,128]{1,0:T(8,128)S(1)} %bitcast.30, f32[16,256]{1,0:T(8,128)S(1)} %get-tuple-element.41.tr_ref, f32[16,256]{1,0:T(8,128)S(1)} %copy-done.5, bf16[16,256,256]{2,1,0:T(8,128)(2,1)S(1)} %copy-done.3, bf16[16,256,256]{2,1,0:T(8,128)(2,1)} %lab_ref.3), custom_call_target="tpu_custom_call" | custom-call | tf_op jit(solution)/shard_map/table/pallas_call | solution.py:383
  (2 shorter events, 0.0 us)
Async XLA Ops:
  0.6 0.9 copy-start.4
  1.5 0.7 copy-start.6
  2.2 0.7 copy-start.7
  2.9 0.7 copy-start.9
  3.6 0.7 copy-start.10
  10.3 1.4 copy-start.1
  11.7 11.5 %copy-start.8 = (s32[16]{0:T(128)S(1)}, s32[16]{0:T(128)}, u32[]{:S(2)}) copy-start(s32[16]{0:T(128)} %counts_ref.3) | copy-start | bytes 196
  11.7 44.8 %all-to-all-start.1 = ((bf16[128,72,128]{2,1,0:T(8,128)(2,1)}), bf16[128,72,128]{2,1,0:T(8,128)(2,1)S(1)}, u32[]{:S(2)}, u32[]{:S(2)}) async-start(bf16[128,72,128]{2,1,0:T(8,128)(2,1)} %bitcast.29), calls=%async_computation.1 | async-start | bytes 4718592 | tf_op jit(solution)/shard_map/all_to_all | solution.py:321
  70.2 1.4 copy-start
  71.6 1.3 copy-start.2
  72.9 37.9 %all-to-all-start.2 = ((bf16[128,72,128]{2,1,0:T(8,128)(2,1)}), bf16[128,72,128]{2,1,0:T(8,128)(2,1)S(1)}, u32[]{:S(2)}, u32[]{:S(2)}) async-start(bf16[128,72,128]{2,1,0:T(8,128)(2,1)} %bitcast.28), calls=%async_computation.2 | async-start | bytes 4718592 | tf_op jit(solution)/shard_map/all_to_all | solution.py:321
  127.4 14.3 %copy-start.3 = (bf16[16,256,256]{2,1,0:T(8,128)(2,1)S(1)}, bf16[16,256,256]{2,1,0:T(8,128)(2,1)}, u32[]{:S(2)}) copy-start(bf16[16,256,256]{2,1,0:T(8,128)(2,1)} %copy-done.2) | copy-start | bytes 6291460
  127.4 14.3 %copy-start.5 = (f32[16,256]{1,0:T(8,128)S(1)}, f32[16,256]{1,0:T(8,128)}, u32[]{:S(2)}) copy-start(f32[16,256]{1,0:T(8,128)} %acc_ref.1) | copy-start | bytes 49156
  127.4 14.2 %all-to-all-start.3 = ((f32[128,1,128]{2,1,0:T(1,128)}), f32[128,1,128]{2,1,0:T(1,128)S(1)}, u32[]{:S(2)}, u32[]{:S(2)}) async-start(f32[128,1,128]{2,1,0:T(1,128)} %bitcast.16), calls=%async_computation.3 | async-start | bytes 131072 | tf_op jit(solution)/shard_map/all_to_all | solution.py:321
where the time goes:
time: 156 us; the launch traced here: 155 us
  waiting for transfers between devices  74.4 us (48%)
  Pallas kernels  49.8 us (32%)
  starting transfers between devices  20.6 us (13%)
  local copies, waits for them, and re-layouts  8.4 us (5%)
    all_to_all x3, waiting for transfers between devices, exchange(): return lax.all_to_all(x, 'shard', split_axis=0, concat_axis=0, tiled=True)  74.4 us
    all_to_all x3, starting transfers between devices, exchange(): return lax.all_to_all(x, 'shard', split_axis=0, concat_axis=0, tiled=True)  20.6 us
    pallas_call x1, Pallas kernels, shards(): pl.pallas_call(combine_kernel, out_shape=shape(256, 256), in_specs=[VMEM]...  14.5 us
    pallas_call x1, Pallas kernels, shards(): pl.pallas_call(owner_kernel, out_shape=(shape(16, 256, 256, dtype=bf16),...  13.7 us
    pallas_call x1, Pallas kernels, shards(): pl.pallas_call(table_kernel, grid=(16,), out_shape=(shape(16, 256, 256),...  13.6 us
    unnamed x22, local copies, waits for them, and re-layouts  7.8 us
    pallas_call x1, Pallas kernels, shards(): pl.pallas_call(route_kernel, out_shape=(shape(rows, 128, dtype=bf16), sha...  5.97 us
  transfers between devices with their start and end apart: 3, of which 3 were waited for; matrix products, arithmetic and copies ran while one was open for 1% of the time, Pallas kernels for 0%

commit v1 on v0

v1 whole, which is shorter than its diff:
```python
import jax
import jax.numpy as jnp
from jax import lax
from jax.experimental import pallas as pl
from jax.experimental.pallas import tpu as pltpu
from jax.sharding import PartitionSpec as P

STEP_RATE = 0.1
DEVS = 128
GROUP = 8
SLOTS = 32
CHUNK = 72
BLOCK = GROUP * CHUNK
NGROUPS = DEVS // GROUP
f32 = jnp.float32
bf16 = jnp.bfloat16
i32 = jnp.int32


def iota(shape, dim):
    return lax.broadcasted_iota(i32, shape, dim)


def one(mask):
    return jnp.where(mask, 1.0, 0.0).astype(bf16)


def dot(a, b, ca=1, cb=0):
    return lax.dot_general(a, b, (((ca,), (cb,)), ((), ())), preferred_element_type=f32)


def pieces_of(x):
    hi = x.astype(bf16).astype(f32)
    rest = x - hi
    mid = rest.astype(bf16).astype(f32)
    return hi, mid, rest - mid


def total(x):
    return jnp.sum(x, axis=0, keepdims=True)


def to_rows(rows, extra):
    left = rows[:, :128].reshape(GROUP, SLOTS, 128)
    right = rows[:, 128:].reshape(GROUP, SLOTS, 128)
    return jnp.concatenate([left, right, extra], axis=1).reshape(BLOCK, 128).astype(bf16)


def from_rows(ref, group):
    block = ref[pl.ds(pl.multiple_of(group * BLOCK, BLOCK), BLOCK), :]
    return block.astype(f32).reshape(GROUP, CHUNK, 128)


def slot_rows(block):
    left = block[:, :SLOTS].reshape(GROUP * SLOTS, 128)
    right = block[:, SLOTS : 2 * SLOTS].reshape(GROUP * SLOTS, 128)
    return jnp.concatenate([left, right], axis=1).astype(bf16)


def send_block(scr, out, sems, g):
    at = pl.ds(pl.multiple_of(g * BLOCK, BLOCK), BLOCK)
    return pltpu.make_async_copy(scr.at[at, :], out.at[at, :], sems.at[g])


def route_kernel(
    cl_any, place_any, pick_any, row_any, q_any, send_any, sid_ref,
    cl_ref, place_ref, pick_ref, row_ref, q_ref, send_ref, ext_scr, in_sems, out_sems,
):
    pairs = [(cl_any, cl_ref), (place_any, place_ref), (pick_any, pick_ref), (row_any, row_ref), (q_any, q_ref)]
    copies = [pltpu.make_async_copy(a, b, in_sems.at[n]) for n, (a, b) in enumerate(pairs)]
    for copy in copies:
        copy.start()
    for copy in copies:
        copy.wait()
    c = cl_ref[...]
    ch, cl = c >> 7, c & 127
    place = place_ref[...]
    table = jnp.concatenate([(place >> 4).astype(f32), (place & 15).astype(f32)], axis=0).astype(bf16)
    i128, i16, i32s = iota((128, 256), 0), iota((16, 256), 0), iota((32, 256), 0)
    query = iota((1, 256), 1)
    queryf = query.astype(f32)
    ds, ls, ohs = [], [], []
    acc = jnp.zeros((32, 128), f32)
    for k in range(8):
        got = dot(table, one(i128 == cl[k : k + 1]))
        mine = i16 == ch[k : k + 1]
        d = total(jnp.where(mine, got[:16], 0.0)).astype(i32)
        l = total(jnp.where(mine, got[16:], 0.0)).astype(i32)
        oh = one(i128 == d)
        is_l = i16 == l
        named = jnp.concatenate([jnp.where(is_l, 1.0, 0.0), jnp.where(is_l, queryf, 0.0)], axis=0)
        acc = acc + dot(named.astype(bf16), oh, 1, 1)
        ds.append(d)
        ls.append(l)
        ohs.append(oh)
    count = acc[:16]
    middle = jnp.where(count > 1.5, jnp.floor(acc[16:] * 0.5), 255.0).astype(bf16)
    rls, sids = [], []
    for k in range(8):
        got = dot(middle, ohs[k])
        border = total(jnp.where(i16 == ls[k], got, 0.0)).astype(i32)
        rl = jnp.where(query > border, 16, 0) + ls[k]
        rls.append(rl)
        sids.append(ds[k] * SLOTS + rl)
    pick = pick_ref[...]
    dp = jnp.zeros((1, 256), i32)
    rlp = jnp.zeros((1, 256), i32)
    for k in range(8):
        dp = jnp.where(pick == k, ds[k], dp)
        rlp = jnp.where(pick == k, rls[k], rlp)
    ohp = one(i128 == dp)
    before = one(iota((256, 256), 0) < iota((256, 256), 1))
    j = total(ohp.astype(f32) * dot(ohp, before)).astype(i32)
    w_t = jnp.where(i32s == rlp, (row_ref[...] + 1).astype(f32), 0.0)
    w_j = jnp.where(i32s == j, (rlp + 1).astype(f32), 0.0)
    res = dot(jnp.concatenate([w_t, w_j, jnp.ones((8, 256), f32)], axis=0).astype(bf16), ohp, 1, 1)
    want = res[64:65]
    free = jnp.where(jnp.concatenate([count, count - 1.0], axis=0) < 0.5, 1.0, 0.0)
    lower = one(iota((32, 32), 1) < iota((32, 32), 0))
    turn = dot(lower, free.astype(bf16))
    turn = jnp.where(free > 0.5, turn, 99.0)
    code = jnp.zeros((32, 128), f32)
    for s in range(SLOTS):
        code = jnp.where(turn == float(s), res[32 + s : 33 + s], code)
    short = jnp.max(jnp.where(want > total(free), 1.0, 0.0), axis=1, keepdims=True)
    got = dot(turn.astype(bf16), ohp)
    carrier = total(jnp.where(got == j.astype(f32), i32s.astype(f32), 0.0)).astype(i32)
    ext = jnp.concatenate([res[:32], code, jnp.broadcast_to(short, (64, 128))], axis=0)
    ext_scr[...] = ext.T
    sid_ref[...] = jnp.concatenate(
        sids + [dp * SLOTS + carrier, dp * SLOTS + rlp] + [jnp.zeros((1, 256), i32)] * 6, axis=0
    )

    sub = iota((16, 256), 0)

    def group(g, _):
        named = [sid_ref[k : k + 1, :] - g * 256 for k in range(8)]
        strips = []
        for i in range(16):
            mask = sub == named[0] - 16 * i
            for k in range(1, 8):
                mask = mask | (sub == named[k] - 16 * i)
            strips.append(one(mask))
        rows = dot(jnp.concatenate(strips, axis=0), q_ref[...])
        extra = ext_scr[pl.ds(pl.multiple_of(g * GROUP, GROUP), GROUP), :]
        extra = jnp.broadcast_to(extra[:, None, :], (GROUP, 8, 128))
        send_ref[pl.ds(pl.multiple_of(g * BLOCK, BLOCK), BLOCK), :] = to_rows(rows, extra)
        send_block(send_ref, send_any, out_sems, g).start()
        return 0

    lax.fori_loop(0, NGROUPS, group, 0, unroll=16)
    for g in range(NGROUPS):
        send_block(send_ref, send_any, out_sems, g).wait()


def slot_major(x):
    second = pltpu.roll(x, 112, 1)
    both = jnp.concatenate(
        [x.reshape(NGROUPS, 1, GROUP, 128), second.reshape(NGROUPS, 1, GROUP, 128)], axis=1
    )
    return both.reshape(256, 128)


def owner_kernel(
    counts_ref, cc_ref, recv_ref, lab_any, x_any, tr_ref, flag_ref, stat_ref, send_any,
    x_ref, lab_ref, send_ref, ext_scr, part_scr, pos_scr, back_scr, lab_sem, x_sem, out_sems,
):
    lab_copy = pltpu.make_async_copy(lab_any, lab_ref, lab_sem)
    lab_copy.start()
    r256, c256 = iota((256, 256), 0), iota((256, 256), 1)
    sent = (r256 & 7) * 32 + ((r256 >> 3) & 1) * 16 + (r256 >> 4)
    perm = one(c256 == sent)

    def gather(g, _):
        block = from_rows(recv_ref, g)
        x = dot(perm, slot_rows(block)).astype(bf16)
        for l in range(16):
            x_ref[l, pl.ds(pl.multiple_of(g * 16, 16), 16), :] = x[l * 16 : (l + 1) * 16]
        ext_scr[pl.ds(pl.multiple_of(g * 64, 64), 64), :] = block[:, 64:72].reshape(64, 128)
        return 0

    lax.fori_loop(0, NGROUPS, gather, 0, unroll=4)
    x_copy = pltpu.make_async_copy(x_ref, x_any, x_sem)
    x_copy.start()
    ext = ext_scr[pl.ds(0, 128, stride=8), :]
    flag_ref[0, 0] = jnp.max(ext[:, 64:65])
    raw = slot_major(ext) - 1.0
    cc = cc_ref[...]
    tr_ref[...] = jnp.where(raw > -0.5, raw - cc * jnp.floor((raw + 0.5) / cc), -1.0)
    stat_ref[...] = jnp.zeros((256, 128), f32)
    lab_copy.wait()
    lane, wide = iota((16, 128), 1), iota((16, 256), 1)
    widef = wide.astype(f32)

    def cluster(l, _):
        lab = lab_ref[l]
        score = dot(x_ref[l], lab, 1, 1)
        valid = wide < counts_ref[l]
        weights, hits = [], []
        for i in range(16):
            at = slice(16 * i, 16 * i + 16)
            s = score[at]
            masked = jnp.where(valid, s, -jnp.inf)
            top = jnp.max(masked, axis=1, keepdims=True)
            weight = jnp.exp(masked - top)
            target = jnp.sum(jnp.where(lane == l, tr_ref[at, :], 0.0), axis=1, keepdims=True)
            hit = widef == target
            stat = jnp.where(lane == l, top, stat_ref[at, :])
            stat = jnp.where(lane == l + 16, jnp.sum(weight, axis=1, keepdims=True), stat)
            found = jnp.sum(jnp.where(hit, s, 0.0), axis=1, keepdims=True)
            stat_ref[at, :] = jnp.where(lane == l + 32, found, stat)
            weights.append(weight.astype(bf16))
            hits.append(one(hit))
        part_scr[l] = dot(jnp.concatenate(weights, axis=0), lab).astype(bf16)
        pos_scr[l] = dot(jnp.concatenate(hits, axis=0), lab).astype(bf16)
        return 0

    lax.fori_loop(0, 16, cluster, 0, unroll=4)
    hi, mid, lo = pieces_of(stat_ref[...])
    first = (hi + pltpu.roll(mid, 64, 1)).reshape(NGROUPS, 2, GROUP, 128)
    second = lo.reshape(NGROUPS, 2, GROUP, 128)
    back_scr[...] = jnp.zeros((1024, 128), f32)
    for r in range(2):
        back_scr[pl.ds(2 * r, 128, stride=8), :] = first[:, r].reshape(128, 128)
        back_scr[pl.ds(2 * r + 1, 128, stride=8), :] = second[:, r].reshape(128, 128)

    back = ((wide & 7) * 32 + ((wide >> 3) & 1) * 16 + (wide >> 4)).astype(f32)
    own_row = iota((16, 128), 0)
    sub = iota((16, 1), 0).astype(f32)

    def scatter(g, _):
        at = pl.ds(pl.multiple_of(g * 16, 16), 16)
        parts = jnp.concatenate([part_scr[l, at, :] for l in range(16)], axis=0)
        pos = jnp.concatenate([pos_scr[l, at, :] for l in range(16)], axis=0)
        codes = ext_scr[pl.ds(pl.multiple_of(g * 64, 64), 64), :]
        own, other = [], []
        for i in range(16):
            c = codes[8 * (i // 2) : 8 * (i // 2) + 8]
            c = jnp.concatenate([c, c], axis=0)
            c = jnp.where(lane == 32 + 16 * (i % 2) + own_row, c, 0.0)
            code = jnp.sum(c, axis=1, keepdims=True)
            own.append(one(back == jnp.where(code > 0.5, -1.0, sub + 16.0 * i)))
            other.append(one(back == jnp.where(code > 0.5, code + (32.0 * (i // 2) - 1.0), -1.0)))
        rows = dot(jnp.concatenate(own, axis=0), parts) + dot(jnp.concatenate(other, axis=0), pos)
        extra = back_scr[pl.ds(pl.multiple_of(g * 64, 64), 64), :].reshape(GROUP, 8, 128)
        send_ref[pl.ds(pl.multiple_of(g * BLOCK, BLOCK), BLOCK), :] = to_rows(rows, extra)
        send_block(send_ref, send_any, out_sems, g).start()
        return 0

    lax.fori_loop(0, NGROUPS, scatter, 0, unroll=8)
    x_copy.wait()
    for g in range(NGROUPS):
        send_block(send_ref, send_any, out_sems, g).wait()


def ready_kernel(
    counts_ref, flag_ref, sid_ref, stat_ref, trc_ref, acc_ref, x_any, lab_any,
    mask_ref, acct_ref, top_ref, tr_ref, weight_any, x_ref, lab_ref, weight_ref, sems,
):
    copies = [pltpu.make_async_copy(x_any, x_ref, sems.at[0]), pltpu.make_async_copy(lab_any, lab_ref, sems.at[1])]
    for copy in copies:
        copy.start()
    for copy in copies:
        copy.wait()
    acct_ref[...] = jnp.concatenate([acc_ref[...], jnp.zeros((112, 256), f32)], axis=0).T
    top_ref[...] = stat_ref[...].T[:16]
    r256 = iota((256, 256), 0)
    tr_ref[...] = trc_ref[...].T[:16]
    cols = jnp.concatenate([sid_ref[...].astype(f32), jnp.zeros((112, 256), f32)], axis=0).T
    pos_weight = jnp.where(flag_ref[0, 0] > 0.5, 0.0, -1.0)
    lane = iota((256, 256), 1).astype(f32)

    def step(n, _):
        slot = lane + (n * 256).astype(f32)
        mask = cols[:, 0:1] == slot
        for k in range(1, 8):
            mask = mask | (cols[:, k : k + 1] == slot)
        pos = jnp.where(cols[:, 8:9] == slot, pos_weight, 0.0)
        mask_ref[n] = jnp.where(mask, 1.0, pos).astype(bf16)
        score = dot(lab_ref[n], x_ref[n], 1, 1)
        weight_ref[n] = jnp.where(r256 < counts_ref[n], jnp.exp(score - top_ref[pl.ds(n, 1), :]), 0.0)
        return 0

    lax.fori_loop(0, NGROUPS, step, 0)
    copy = pltpu.make_async_copy(weight_ref, weight_any, sems.at[0])
    copy.start()
    copy.wait()


def lse_kernel(recv_ref, sid_ref, loss_ref, send_ref, lse_ref, top_ref, ext_scr):
    def take(g, _):
        block = from_rows(recv_ref, g)
        ext_scr[pl.ds(pl.multiple_of(g * 64, 64), 64), :] = block[:, 64:72].reshape(64, 128)
        return 0

    lax.fori_loop(0, NGROUPS, take, 0, unroll=2)
    stats = []
    for r in range(2):
        first = ext_scr[pl.ds(2 * r, 128, stride=8), :]
        second = ext_scr[pl.ds(2 * r + 1, 128, stride=8), :]
        stats.append(first + pltpu.roll(first, 64, 1) + second)
    lane = iota((128, 128), 1)
    tops_r = jnp.where(lane < 16, stats[0], pltpu.roll(stats[1], 16, 1))
    top_ref[...] = jnp.where(lane < 32, tops_r, 0.0)
    both = jnp.where(lane < 64, stats[0], pltpu.roll(stats[1], 64, 1)).T
    table = jnp.concatenate(pieces_of(both), axis=0).astype(bf16)
    i128, i16, i32s = iota((128, 256), 0), iota((16, 256), 0), iota((32, 256), 0)
    sid = sid_ref[...]
    tops, sums, ohs = [], [], []
    target = jnp.zeros((1, 256), f32)
    for k in range(8):
        s = sid[k : k + 1]
        oh = one(i128 == (s >> 5))
        got = dot(table, oh)
        got = got[:128] + got[128:256] + got[256:]
        got = jnp.where((s & 16) == 0, got[:48], got[64:112])
        mine = i16 == (s & 15)
        tops.append(total(jnp.where(mine, got[:16], 0.0)))
        sums.append(total(jnp.where(mine, got[16:32], 0.0)))
        target = target + total(jnp.where(mine, got[32:48], 0.0))
        ohs.append(oh)
    largest = tops[0]
    for k in range(1, 8):
        largest = jnp.maximum(largest, tops[k])
    norm = sums[0] * jnp.exp(tops[0] - largest)
    for k in range(1, 8):
        norm = norm + sums[k] * jnp.exp(tops[k] - largest)
    lse = largest + jnp.log(norm)
    loss_ref[...] = lse - target
    lse_ref[...] = jnp.broadcast_to(lse, (8, 256))
    split = pieces_of(lse)
    out = jnp.zeros((96, 128), f32)
    for k in range(8):
        mine = i32s == (sid[k : k + 1] & 31)
        w = jnp.concatenate([jnp.where(mine, p, 0.0) for p in split], axis=0)
        out = out + dot(w.astype(bf16), ohs[k], 1, 1)
    out = out[:32] + out[32:64] + out[64:]
    send_ref[...] = jnp.concatenate([out, jnp.zeros((96, 128), f32)], axis=0).T


def combine_kernel(recv_ref, mask_ref, lse_ref, top_ref, late_ref, out_ref, top_scr):
    lse = jnp.concatenate([lse_ref[...]] * 16, axis=0).T
    lse = jnp.concatenate([lse, lse], axis=1)
    r256, c256 = iota((128, 256), 0), iota((128, 256), 1)
    spread = one((r256 == (c256 & 31)) & (r256 < 32))
    wide = jnp.zeros((128, 256), f32)
    for piece in pieces_of(top_ref[...]):
        wide = wide + dot(piece.astype(bf16), spread)
    wide = jnp.where((r256 & 7) == (c256 >> 5), wide, 0.0)
    top_scr[...] = jnp.sum(wide.reshape(NGROUPS, GROUP, 256), axis=1)

    def group(g, acc):
        rows = slot_rows(from_rows(recv_ref, g))
        top = top_scr[pl.ds(g, 1), :]
        his, los = [], []
        for i in range(16):
            at = slice(16 * i, 16 * i + 16)
            mask = mask_ref[g, at, :].astype(f32)
            a = jnp.where(mask > 0.5, jnp.exp(top - lse[at]), mask)
            hi = a.astype(bf16)
            his.append(hi)
            los.append((a - hi.astype(f32)).astype(bf16))
        return acc + (dot(jnp.concatenate(his, axis=0), rows) + dot(jnp.concatenate(los, axis=0), rows))

    total_grad = lax.fori_loop(0, NGROUPS, group, -late_ref[...], unroll=8)
    out_ref[...] = total_grad.astype(bf16)


PART = 4


def table_kernel(
    lse_ref, top_ref, tr_ref, acct_ref, weight_any, x_any, lab_any, new_any, nacc_ref,
    weight_ref, x_ref, lab_ref, fac_scr, new_scr, out_scr, in_sems, out_sems,
):
    def inputs_of(p):
        at = pl.ds(p * PART, PART)
        pairs = [(weight_any, weight_ref), (x_any, x_ref), (lab_any, lab_ref)]
        return [pltpu.make_async_copy(a.at[at], b.at[at], in_sems.at[n, p]) for n, (a, b) in enumerate(pairs)]

    def output_of(p):
        at = pl.ds(p * PART, PART)
        return pltpu.make_async_copy(new_scr.at[at], new_any.at[at], out_sems.at[p])

    for p in range(16 // PART):
        for copy in inputs_of(p):
            copy.start()
    fac_scr[...] = jnp.exp(top_ref[...] - slot_major(lse_ref[...]).T[:16])
    out_scr[...] = jnp.zeros((256, 128), f32)
    rowf = iota((16, 256), 0).astype(f32)
    lane = iota((16, 128), 1)

    def part(p, _):
        for copy in inputs_of(p):
            copy.wait()
        for q in range(PART):
            l = p * PART + q
            fac = fac_scr[pl.ds(l, 1), :]
            target = tr_ref[pl.ds(l, 1), :]
            strips = []
            for i in range(16):
                hit = rowf == target - 16.0 * i
                strips.append((weight_ref[l, 16 * i : 16 * i + 16, :] * fac - jnp.where(hit, 1.0, 0.0)).astype(bf16))
            grad = dot(jnp.concatenate(strips, axis=0), x_ref[l])
            for i in range(16):
                at = slice(16 * i, 16 * i + 16)
                g = grad[at]
                square = g * g
                both = (square[:, :128] + square[:, 128:]) * (1.0 / 256.0)
                both = both + jnp.where(lane == l, acct_ref[at, :], 0.0)
                accum = jnp.sum(both, axis=1, keepdims=True)
                new_scr[l, at, :] = lab_ref[l, at, :].astype(f32) - g * (STEP_RATE / jnp.sqrt(accum))
                out_scr[at, :] = jnp.where(lane == l, accum, out_scr[at, :])
        output_of(p).start()
        return 0

    lax.fori_loop(0, 16 // PART, part, 0)
    nacc_ref[...] = out_scr[...].T[:16]
    for p in range(16 // PART):
        output_of(p).wait()


def params(mib):
    return pltpu.CompilerParams(vmem_limit_bytes=mib * 1024 * 1024)


def shape(*dims, dtype=f32):
    return jax.ShapeDtypeStruct(dims, dtype)


VMEM = pl.BlockSpec(memory_space=pltpu.VMEM)
SMEM = pl.BlockSpec(memory_space=pltpu.SMEM)
HBM = pl.BlockSpec(memory_space=pltpu.HBM)


def in_hbm(x):
    return pltpu.with_memory_space_constraint(x, pltpu.HBM)


def exchange(x):
    return lax.all_to_all(x, "shard", split_axis=0, concat_axis=0, tiled=True)


def shards(queries, clusters, placement, pos_pick, pos_row, counts, labels, accum):
    rows = DEVS * CHUNK
    send, sid = pl.pallas_call(
        route_kernel,
        out_shape=(pltpu.HBM((rows, 128), bf16), pltpu.VMEM((16, 256), i32)),
        in_specs=[HBM] * 5,
        out_specs=(HBM, VMEM),
        scratch_shapes=[
            pltpu.VMEM((8, 256), i32),
            pltpu.VMEM((16, 128), i32),
            pltpu.VMEM((1, 256), i32),
            pltpu.VMEM((1, 256), i32),
            pltpu.VMEM((256, 256), bf16),
            pltpu.VMEM((rows, 128), bf16),
            pltpu.VMEM((128, 128), f32),
            pltpu.SemaphoreType.DMA((5,)),
            pltpu.SemaphoreType.DMA((NGROUPS,)),
        ],
        compiler_params=params(16),
        name="route",
    )(
        in_hbm(clusters.T), in_hbm(placement.reshape(16, 128)), in_hbm(pos_pick.reshape(1, 256)),
        in_hbm(pos_row.reshape(1, 256)), in_hbm(queries),
    )
    recv = exchange(send)
    lanes = jnp.concatenate([counts.astype(f32), jnp.ones((112,), f32)]).reshape(1, 128)
    x, slot_target, flag, stat, send = pl.pallas_call(
        owner_kernel,
        out_shape=(
            pltpu.HBM((16, 256, 256), bf16), pltpu.VMEM((256, 128), f32), shape(1, 1), pltpu.VMEM((256, 128), f32),
            pltpu.HBM((rows, 128), bf16),
        ),
        in_specs=[SMEM, VMEM, VMEM, HBM],
        out_specs=(HBM, VMEM, SMEM, VMEM, HBM),
        scratch_shapes=[
            pltpu.VMEM((16, 256, 256), bf16),
            pltpu.VMEM((16, 256, 256), bf16),
            pltpu.VMEM((rows, 128), bf16),
            pltpu.VMEM((1024, 128), f32),
            pltpu.VMEM((16, 256, 256), bf16),
            pltpu.VMEM((16, 256, 256), bf16),
            pltpu.VMEM((1024, 128), f32),
            pltpu.SemaphoreType.DMA,
            pltpu.SemaphoreType.DMA,
            pltpu.SemaphoreType.DMA((NGROUPS,)),
        ],
        compiler_params=params(24),
        name="owner",
    )(counts, lanes, recv, in_hbm(labels))

    def with_rows():
        hit = jnp.arange(256, dtype=f32) == slot_target[:, :16].T[:, :, None]
        found = jnp.einsum("csl,clw->csw", hit.astype(bf16), labels, preferred_element_type=f32).astype(bf16)
        found = found.reshape(16, NGROUPS, 2, GROUP, 256).transpose(1, 3, 2, 0, 4).reshape(DEVS * SLOTS, 256)
        return exchange(found)[sid[9]].astype(f32)

    late = lax.cond(flag[0, 0] > 0.5, with_rows, lambda: jnp.zeros((256, 256), f32))
    send, late = lax.optimization_barrier((send, late))
    recv = exchange(send)
    mask, acct, top, target, weight = pl.pallas_call(
        ready_kernel,
        out_shape=(
            pltpu.VMEM((NGROUPS, 256, 256), bf16), pltpu.VMEM((256, 128), f32), pltpu.VMEM((16, 256), f32),
            pltpu.VMEM((16, 256), f32), pltpu.HBM((16, 256, 256), f32),
        ),
        in_specs=[SMEM] * 2 + [VMEM] * 4 + [HBM] * 2,
        out_specs=(VMEM,) * 4 + (HBM,),
        scratch_shapes=[
            pltpu.VMEM((16, 256, 256), bf16),
            pltpu.VMEM((16, 256, 256), bf16),
            pltpu.VMEM((16, 256, 256), f32),
            pltpu.SemaphoreType.DMA((2,)),
        ],
        compiler_params=params(16),
        cost_estimate=pl.CostEstimate(flops=2 * 16 * 256**3, bytes_accessed=10_000_000, transcendentals=16 * 256**2),
        name="ready",
    )(counts, flag, sid, stat, slot_target, accum, in_hbm(x), in_hbm(labels))
    loss, send, lse, tops = pl.pallas_call(
        lse_kernel,
        out_shape=(shape(1, 256), shape(DEVS, 128), shape(8, 256), shape(DEVS, 128)),
        in_specs=[VMEM, VMEM],
        out_specs=(VMEM,) * 4,
        scratch_shapes=[pltpu.VMEM((1024, 128), f32)],
        compiler_params=params(8),
        name="normalizer",
    )(recv, sid)
    back = exchange(send)
    query_grad = pl.pallas_call(
        combine_kernel,
        out_shape=shape(256, 256, dtype=bf16),
        in_specs=[VMEM] * 5,
        out_specs=VMEM,
        scratch_shapes=[
            pltpu.VMEM((NGROUPS, 256), f32),
        ],
        compiler_params=params(8),
        cost_estimate=pl.CostEstimate(flops=2 * 2 * 256 * 4096 * 256, bytes_accessed=5_000_000, transcendentals=256 * 4096),
        name="combine",
    )(recv, mask, lse, tops, late)
    new_labels, new_accum = pl.pallas_call(
        table_kernel,
        out_shape=(pltpu.HBM((16, 256, 256), f32), shape(16, 256)),
        in_specs=[VMEM] * 4 + [HBM] * 3,
        out_specs=(HBM, VMEM),
        scratch_shapes=[
            pltpu.VMEM((16, 256, 256), f32),
            pltpu.VMEM((16, 256, 256), bf16),
            pltpu.VMEM((16, 256, 256), bf16),
            pltpu.VMEM((16, 256), f32),
            pltpu.VMEM((16, 256, 256), f32),
            pltpu.VMEM((256, 128), f32),
            pltpu.SemaphoreType.DMA((3, 16 // PART)),
            pltpu.SemaphoreType.DMA((16 // PART,)),
        ],
        compiler_params=params(24),
        name="table",
    )(back, top, target, acct, in_hbm(weight), in_hbm(x), in_hbm(labels))

    return (new_labels, new_accum, query_grad, loss.reshape(256))


def solution(mesh):
    return jax.shard_map(
        shards,
        mesh=mesh,
        in_specs=(
            P("shard", None), P("shard", None), P(), P("shard"), P("shard"), P("shard"),
            P("shard", None, None), P("shard", None),
        ),
        out_specs=(P("shard", None, None), P("shard", None), P("shard", None), P("shard")),
        check_vma=False,
    )
```

time: 156 us -> 124 us (0.79)
  waiting for transfers between devices: 74.4 us -> 55.8 us
  Pallas kernels: 49.8 us -> 42.5 us
  local copies, waits for them, and re-layouts: 8.4 us -> 2.97 us
    all_to_all x3, waiting for transfers between devices: 74.4 us -> 55.8 us  [exchange(): return lax.all_to_all(x, 'shard', split_axis=0, concat_axis=0, tiled=True)]
    pallas_call x4 -> x5, Pallas kernels: 47.8 us -> 40.5 us  [the longest x1 14.6 us: shards(): pl.pallas_call(ready_kernel, out_shape=(pltpu.VMEM((NGROUPS, 256, 256), b...]
    unnamed x22 -> x8, local copies, waits for them, and re-layouts: 7.8 us -> 2.95 us
  transfers between devices with their start and end apart: 3 -> 3, of which waited for: 3 -> 3; matrix products, arithmetic and copies ran while one was open for 1% -> 0% of each run, Pallas kernels for 0% -> 14%
where the time goes in v1:
time: 124 us; the launch traced here: 123 us
  waiting for transfers between devices  55.8 us (45%)
  Pallas kernels  42.5 us (34%)
  starting transfers between devices  20.4 us (16%)
  local copies, waits for them, and re-layouts  2.97 us (2%)
  between operations  1.56 us (1%)
    all_to_all x3, waiting for transfers between devices, exchange(): return lax.all_to_all(x, 'shard', split_axis=0, concat_axis=0, tiled=True)  55.8 us
    all_to_all x3, starting transfers between devices, exchange(): return lax.all_to_all(x, 'shard', split_axis=0, concat_axis=0, tiled=True)  20.4 us
    pallas_call x1, Pallas kernels, shards(): pl.pallas_call(ready_kernel, out_shape=(pltpu.VMEM((NGROUPS, 256, 256), b...  14.6 us
    pallas_call x1, Pallas kernels, shards(): pl.pallas_call(owner_kernel, out_shape=(pltpu.HBM((16, 256, 256), bf16),...  10.1 us
    pallas_call x1, Pallas kernels, shards(): pl.pallas_call(route_kernel, out_shape=(pltpu.HBM((rows, 128), bf16), plt...  6.67 us
    pallas_call x1, Pallas kernels, shards(): pl.pallas_call(table_kernel, out_shape=(pltpu.HBM((16, 256, 256), f32), s...  6.28 us
    unnamed x8, local copies, waits for them, and re-layouts  2.95 us
    pallas_call x1, Pallas kernels, shards(): pl.pallas_call(combine_kernel, out_shape=shape(256, 256, dtype=bf16), in_...  2.8 us
  transfers between devices with their start and end apart: 3, of which 3 were waited for; matrix products, arithmetic and copies ran while one was open for 0% of the time, Pallas kernels for 14%

profile of v1, /device:TPU:1, one launch (start us, length us, event | category | flops | bytes accessed | tf_op | source)
XLA Modules:
  0.0 123.4 jit_solution(3145040010506070948)
XLA Ops:
  0.6 6.7 %route.1 = (bf16[9216,128]{1,0:T(8,128)(2,1)}, s32[16,256]{1,0:T(8,128)S(1)}) custom-call(s32[8,256]{1,0:T(8,128)} %bitcast.35, s32[16,128]{1,0:T(8,128)} %bitcast.36, s32[1,256]{1,0:T(1,128)} %bitcast.38, s32[1,256]{1,0:T(1,128)} %bitcast.39, bf16[256,256]{1,0:T(8,128)(2,1)} %q_any.1), custom_call_target="tpu_custom_call" | custom-call | tf_op jit(solution)/shard_map/route/pallas_call | solution.py:446
  7.3 0.0 copy-start.3
  7.3 11.5 %all-to-all-start.1 = ((bf16[128,72,128]{2,1,0:T(8,128)(2,1)}), bf16[128,72,128]{2,1,0:T(8,128)(2,1)S(1)}, u32[]{:S(2)}, u32[]{:S(2)}) async-start(bf16[128,72,128]{2,1,0:T(8,128)(2,1)} %bitcast.33), calls=%async_computation.1 | async-start | bytes 4718592 | tf_op jit(solution)/shard_map/all_to_all | solution.py:441
  18.8 0.0 copy-done.3
  18.9 33.2 %all-to-all-done.1 = bf16[128,72,128]{2,1,0:T(8,128)(2,1)S(1)} async-done(((bf16[128,72,128]{2,1,0:T(8,128)(2,1)}), bf16[128,72,128]{2,1,0:T(8,128)(2,1)S(1)}, u32[]{:S(2)}, u32[]{:S(2)}) %all-to-all-start.1) | async-done | bytes 2359328 | tf_op jit(solution)/shard_map/all_to_all | solution.py:441
  52.1 10.1 %owner.1 = (bf16[16,256,256]{2,1,0:T(8,128)(2,1)}, f32[256,128]{1,0:T(8,128)S(1)}, f32[1,1]{1,0:T(1,128)}, f32[256,128]{1,0:T(8,128)S(1)}, bf16[9216,128]{1,0:T(8,128)(2,1)}) custom-call(s32[16]{0:T(128)S(1)} %copy-done.3, f32[1,128]{1,0:T(1,128)S(1)} %pad_bitcast_fusion.cc_ref, bf16[9216,128]{1,0:T(8,128)(2,1)S(1)} %bitcast.29, bf16[16,256,256]{2,1,0:T(8,128)(2,1)} %lab_any.5), custom_call_target="tpu_custom_call" | custom-call | tf_op jit(solution)/shard_map/owner/pallas_call | solution.py:470
  62.9 0.0 copy-start.2
  62.9 4.5 %all-to-all-start.2 = ((bf16[128,72,128]{2,1,0:T(8,128)(2,1)}), bf16[128,72,128]{2,1,0:T(8,128)(2,1)S(1)}, u32[]{:S(2)}, u32[]{:S(2)}) async-start(bf16[128,72,128]{2,1,0:T(8,128)(2,1)} %bitcast.32), calls=%async_computation.2 | async-start | bytes 4718592 | tf_op jit(solution)/shard_map/all_to_all | solution.py:441
  67.5 0.0 copy-done.2
  67.5 14.6 %ready.1 = (bf16[16,256,256]{2,1,0:T(8,128)(2,1)S(1)}, f32[256,128]{1,0:T(8,128)S(1)}, f32[16,256]{1,0:T(8,128)S(1)}, f32[16,256]{1,0:T(8,128)S(1)}, f32[16,256,256]{2,1,0:T(8,128)}) custom-call(s32[16]{0:T(128)S(1)} %copy-done.3, f32[1,1]{1,0:T(1,128)} %get-tuple-element.38.flag_ref, s32[16,256]{1,0:T(8,128)S(1)} %get-tuple-element.40.sid_ref, ...), custom_call_target="tpu_custom_call" | custom-call | flops 536870912 | bytes 10000000 | tf_op jit(solution)/shard_map/ready/pallas_call | solution.py:503
  82.1 0.0 copy-start
  82.1 1.4 %copy-done = bf16[16,256,256]{2,1,0:T(8,128)(2,1)} copy-done((bf16[16,256,256]{2,1,0:T(8,128)(2,1)}, bf16[16,256,256]{2,1,0:T(8,128)(2,1)S(1)}, u32[]{:S(2)}) %copy-start) | copy-done | bytes 2097176
  83.4 17.4 %all-to-all-done.2 = bf16[128,72,128]{2,1,0:T(8,128)(2,1)S(1)} async-done(((bf16[128,72,128]{2,1,0:T(8,128)(2,1)}), bf16[128,72,128]{2,1,0:T(8,128)(2,1)S(1)}, u32[]{:S(2)}, u32[]{:S(2)}) %all-to-all-start.2) | async-done | bytes 2359328 | tf_op jit(solution)/shard_map/all_to_all | solution.py:441
  100.9 2.1 %normalizer.1 = (f32[1,256]{1,0:T(1,128)}, f32[128,128]{1,0:T(8,128)}, f32[8,256]{1,0:T(8,128)S(1)}, f32[128,128]{1,0:T(8,128)S(1)}) custom-call(bf16[9216,128]{1,0:T(8,128)(2,1)S(1)} %bitcast.27, s32[16,256]{1,0:T(8,128)S(1)} %get-tuple-element.40.sid_ref), custom_call_target="tpu_custom_call" | custom-call | tf_op jit(solution)/shard_map/normalizer/pallas_call | solution.py:521
  102.9 4.4 %all-to-all-start.3 = ((f32[128,1,128]{2,1,0:T(1,128)}), f32[128,1,128]{2,1,0:T(1,128)S(1)}, u32[]{:S(2)}, u32[]{:S(2)}) async-start(f32[128,1,128]{2,1,0:T(1,128)} %bitcast.18), calls=%async_computation.3 | async-start | bytes 131072 | tf_op jit(solution)/shard_map/all_to_all | solution.py:441
  107.4 0.0 copy-start.1
  107.4 1.6 %copy-done.1 = bf16[16,256,256]{2,1,0:T(8,128)(2,1)S(1)} copy-done((bf16[16,256,256]{2,1,0:T(8,128)(2,1)S(1)}, bf16[16,256,256]{2,1,0:T(8,128)(2,1)}, u32[]{:S(2)}) %copy-start.1) | copy-done | bytes 2097176
  109.0 2.8 %combine.1 = bf16[256,256]{1,0:T(8,128)(2,1)} custom-call(bf16[9216,128]{1,0:T(8,128)(2,1)S(1)} %bitcast.28, bf16[16,256,256]{2,1,0:T(8,128)(2,1)S(1)} %copy-done.1, f32[8,256]{1,0:T(8,128)S(1)} %get-tuple-element.52.lse_ref, f32[128,128]{1,0:T(8,128)S(1)} %get-tuple-element.53.top_ref, f32[256,256]{1,0:T(8,128)S(1)} %get-tuple-element.65.late_ref), custom_call_target="tpu_custom_call" | custom-call | flops 1073741824 | bytes 5000000 | tf_op jit(solution)/shard_map/combine/pallas_call | solution.py:531
  111.8 5.2 %all-to-all-done.3 = f32[128,1,128]{2,1,0:T(1,128)S(1)} async-done(((f32[128,1,128]{2,1,0:T(1,128)}), f32[128,1,128]{2,1,0:T(1,128)S(1)}, u32[]{:S(2)}, u32[]{:S(2)}) %all-to-all-start.3) | async-done | bytes 65568 | tf_op jit(solution)/shard_map/all_to_all | solution.py:441
  116.9 6.3 %table.1 = (f32[16,256,256]{2,1,0:T(8,128)}, f32[16,256]{1,0:T(8,128)}) custom-call(f32[128,128]{1,0:T(8,128)S(1)} %bitcast.30, f32[16,256]{1,0:T(8,128)S(1)} %get-tuple-element.45.top_ref, f32[16,256]{1,0:T(8,128)S(1)} %get-tuple-element.46.tr_ref, f32[256,128]{1,0:T(8,128)S(1)} %get-tuple-element.47.acct_ref, ...), custom_call_target="tpu_custom_call" | custom-call | tf_op jit(solution)/shard_map/table/pallas_call | solution.py:543
  (4 shorter events, 0.1 us)
Async XLA Ops:
  7.3 11.5 %copy-start.3 = (s32[16]{0:T(128)S(1)}, s32[16]{0:T(128)}, u32[]{:S(2)}) copy-start(s32[16]{0:T(128)} %counts_ref.3) | copy-start | bytes 196
  7.3 44.8 %all-to-all-start.1 = ((bf16[128,72,128]{2,1,0:T(8,128)(2,1)}), bf16[128,72,128]{2,1,0:T(8,128)(2,1)S(1)}, u32[]{:S(2)}, u32[]{:S(2)}) async-start(bf16[128,72,128]{2,1,0:T(8,128)(2,1)} %bitcast.33), calls=%async_computation.1 | async-start | bytes 4718592 | tf_op jit(solution)/shard_map/all_to_all | solution.py:441
  62.9 4.5 %copy-start.2 = (f32[16,256]{1,0:T(8,128)S(1)}, f32[16,256]{1,0:T(8,128)}, u32[]{:S(2)}) copy-start(f32[16,256]{1,0:T(8,128)} %acc_ref.1) | copy-start | bytes 49156
  62.9 37.9 %all-to-all-start.2 = ((bf16[128,72,128]{2,1,0:T(8,128)(2,1)}), bf16[128,72,128]{2,1,0:T(8,128)(2,1)S(1)}, u32[]{:S(2)}, u32[]{:S(2)}) async-start(bf16[128,72,128]{2,1,0:T(8,128)(2,1)} %bitcast.32), calls=%async_computation.2 | async-start | bytes 4718592 | tf_op jit(solution)/shard_map/all_to_all | solution.py:441
  82.1 1.4 %copy-start = (bf16[16,256,256]{2,1,0:T(8,128)(2,1)}, bf16[16,256,256]{2,1,0:T(8,128)(2,1)S(1)}, u32[]{:S(2)}) copy-start(bf16[16,256,256]{2,1,0:T(8,128)(2,1)S(1)} %get-tuple-element.51.mask_ref) | copy-start | bytes 6291460
  102.9 14.0 %all-to-all-start.3 = ((f32[128,1,128]{2,1,0:T(1,128)}), f32[128,1,128]{2,1,0:T(1,128)S(1)}, u32[]{:S(2)}, u32[]{:S(2)}) async-start(f32[128,1,128]{2,1,0:T(1,128)} %bitcast.18), calls=%async_computation.3 | async-start | bytes 131072 | tf_op jit(solution)/shard_map/all_to_all | solution.py:441
  107.4 1.6 %copy-start.1 = (bf16[16,256,256]{2,1,0:T(8,128)(2,1)S(1)}, bf16[16,256,256]{2,1,0:T(8,128)(2,1)}, u32[]{:S(2)}) copy-start(bf16[16,256,256]{2,1,0:T(8,128)(2,1)} %copy-done) | copy-start | bytes 6291460

commit v2 on v1

v2 whole, which is shorter than its diff:
```python
import jax
import jax.numpy as jnp
from jax import lax
from jax.experimental import pallas as pl
from jax.experimental.pallas import tpu as pltpu
from jax.sharding import PartitionSpec as P

STEP_RATE = 0.1
DEVS = 128
GROUP = 8
SLOTS = 32
PAIRS = 24
OUT = 56
BACK = 64
NGROUPS = DEVS // GROUP
f32 = jnp.float32
bf16 = jnp.bfloat16
i32 = jnp.int32


def iota(shape, dim):
    return lax.broadcasted_iota(i32, shape, dim)


def one(mask):
    return jnp.where(mask, 1.0, 0.0).astype(bf16)


def dot(a, b, ca=1, cb=0):
    return lax.dot_general(a, b, (((ca,), (cb,)), ((), ())), preferred_element_type=f32)


def pieces_of(x):
    hi = x.astype(bf16).astype(f32)
    rest = x - hi
    mid = rest.astype(bf16).astype(f32)
    return hi, mid, rest - mid


def total(x):
    return jnp.sum(x, axis=0, keepdims=True)


def from_rows(ref, group, chunk):
    size = GROUP * chunk
    block = ref[pl.ds(pl.multiple_of(group * size, size), size), :]
    return block.astype(f32).reshape(GROUP, chunk, 128)


def slot_rows(block, slots):
    left = block[:, :slots].reshape(GROUP * slots, 128)
    right = block[:, slots : 2 * slots].reshape(GROUP * slots, 128)
    return jnp.concatenate([left, right], axis=1).astype(bf16)


def send_block(scr, out, sems, g, chunk):
    size = GROUP * chunk
    at = pl.ds(pl.multiple_of(g * size, size), size)
    return pltpu.make_async_copy(scr.at[at, :], out.at[at, :], sems.at[g])


def route_kernel(
    cl_any, place_any, pick_any, row_any, q_any, send_any, sid_ref,
    cl_ref, place_ref, pick_ref, row_ref, q_ref, send_ref, ext_scr, in_sems, out_sems,
):
    pairs = [(cl_any, cl_ref), (place_any, place_ref), (pick_any, pick_ref), (row_any, row_ref), (q_any, q_ref)]
    copies = [pltpu.make_async_copy(a, b, in_sems.at[n]) for n, (a, b) in enumerate(pairs)]
    for copy in copies:
        copy.start()
    for copy in copies:
        copy.wait()
    c = cl_ref[...]
    ch, cl = c >> 7, c & 127
    place = place_ref[...]
    table = jnp.concatenate([(place >> 4).astype(f32), (place & 15).astype(f32)], axis=0).astype(bf16)
    i128, i16, i32s = iota((128, 256), 0), iota((16, 256), 0), iota((32, 256), 0)
    query = iota((1, 256), 1)
    queryf = query.astype(f32)
    ds, ls, ohs = [], [], []
    acc = jnp.zeros((32, 128), f32)
    for k in range(8):
        got = dot(table, one(i128 == cl[k : k + 1]))
        mine = i16 == ch[k : k + 1]
        d = total(jnp.where(mine, got[:16], 0.0)).astype(i32)
        l = total(jnp.where(mine, got[16:], 0.0)).astype(i32)
        oh = one(i128 == d)
        is_l = i16 == l
        named = jnp.concatenate([jnp.where(is_l, 1.0, 0.0), jnp.where(is_l, queryf, 0.0)], axis=0)
        acc = acc + dot(named.astype(bf16), oh, 1, 1)
        ds.append(d)
        ls.append(l)
        ohs.append(oh)
    count = acc[:16]
    middle = jnp.where(count > 1.5, jnp.floor(acc[16:] * 0.5), 255.0).astype(bf16)
    before = one(iota((256, 256), 0) < iota((256, 256), 1))
    used = jnp.zeros((128, 1), f32)
    rls, js, codes = [], [], []
    for k in range(8):
        got = dot(middle, ohs[k])
        border = total(jnp.where(i16 == ls[k], got, 0.0)).astype(i32)
        rl = jnp.where(query > border, 16, 0) + ls[k]
        ohf = ohs[k].astype(f32)
        j = total(ohf * (dot(ohs[k], before) + used)).astype(i32)
        used = used + jnp.sum(ohf, axis=1, keepdims=True)
        codes.append(jnp.where(i32s == j, (rl + 1).astype(f32), 0.0).astype(bf16))
        rls.append(rl)
        js.append(j)
    pick = pick_ref[...]
    dp = jnp.zeros((1, 256), i32)
    rlp = jnp.zeros((1, 256), i32)
    for k in range(8):
        dp = jnp.where(pick == k, ds[k], dp)
        rlp = jnp.where(pick == k, rls[k], rlp)
    ohp = one(i128 == dp)
    ohf = ohp.astype(f32)
    jp = total(ohf * (dot(ohp, before) + used)).astype(i32)
    codes.append(jnp.where(i32s == jp, (rlp + 65).astype(f32), 0.0).astype(bf16))
    code = dot(jnp.concatenate(codes, axis=1), jnp.concatenate(ohs + [ohp], axis=1), 1, 1)
    rows = dot(jnp.where(i32s == rlp, (row_ref[...] + 1).astype(f32), 0.0).astype(bf16), ohp, 1, 1)
    most = used + jnp.sum(ohf, axis=1, keepdims=True)
    full = jnp.where((used > PAIRS + 0.5) | (most > SLOTS - 0.5), 1.0, 0.0)
    full = jnp.max(full, axis=0, keepdims=True)
    ext_scr[...] = jnp.concatenate([code, rows, jnp.broadcast_to(full, (64, 128))], axis=0).T
    sid_ref[...] = jnp.concatenate(
        [d * SLOTS + j for d, j in zip(ds, js)] + rls + [dp * SLOTS + jp] + [jnp.zeros((1, 256), i32)] * 7, axis=0
    )
    sub = iota((8, 256), 0)

    def group(g, _):
        named = [sid_ref[k : k + 1, :] - g * 256 for k in range(8)]
        strips = []
        for i in range(12):
            tiles = []
            for q in (2 * i, 2 * i + 1):
                first = (q // 3) * SLOTS + (q % 3) * 8
                mask = sub == named[0] - first
                for k in range(1, 8):
                    mask = mask | (sub == named[k] - first)
                tiles.append(jnp.where(mask, 1.0, 0.0))
            strips.append(jnp.concatenate(tiles, axis=0).astype(bf16))
        rows = dot(jnp.concatenate(strips, axis=0), q_ref[...])
        left = rows[:, :128].reshape(GROUP, PAIRS, 128)
        right = rows[:, 128:].reshape(GROUP, PAIRS, 128)
        extra = ext_scr[pl.ds(pl.multiple_of(g * GROUP, GROUP), GROUP), :]
        extra = jnp.broadcast_to(extra[:, None, :], (GROUP, 8, 128))
        out = jnp.concatenate([left, right, extra], axis=1).reshape(GROUP * OUT, 128).astype(bf16)
        send_ref[pl.ds(pl.multiple_of(g * GROUP * OUT, GROUP * OUT), GROUP * OUT), :] = out
        send_block(send_ref, send_any, out_sems, g, OUT).start()
        return 0

    lax.fori_loop(0, NGROUPS, group, 0, unroll=16)
    for g in range(NGROUPS):
        send_block(send_ref, send_any, out_sems, g, OUT).wait()


def slot_major(x):
    second = pltpu.roll(x, 112, 1)
    both = jnp.concatenate(
        [x.reshape(NGROUPS, 1, GROUP, 128), second.reshape(NGROUPS, 1, GROUP, 128)], axis=1
    )
    return both.reshape(256, 128)


def owner_kernel(
    counts_ref, cc_ref, recv_ref, lab_any, x_any, tr_ref, flag_ref, stat_ref, send_any,
    x_ref, lab_ref, send_ref, ext_scr, key_scr, part_scr, pos_scr, lab_sem, x_sem, out_sems,
):
    lab_copy = pltpu.make_async_copy(lab_any, lab_ref, lab_sem)
    lab_copy.start()

    def take(g, _):
        block = from_rows(recv_ref, g, OUT)
        ext_scr[pl.ds(pl.multiple_of(g * 64, 64), 64), :] = block[:, 48:56].reshape(64, 128)
        return 0

    lax.fori_loop(0, NGROUPS, take, 0, unroll=16)
    ext = ext_scr[pl.ds(0, 128, stride=8), :]
    flag_ref[0, 0] = jnp.max(ext[:, 64:65])
    source, col = iota((128, 256), 0), iota((128, 256), 1)
    owner_of = jnp.floor((col.astype(f32) + 0.5) / PAIRS).astype(i32)
    spread = one(source == col - owner_of * PAIRS)
    codes = jnp.where((source & 7) == owner_of, dot(ext.astype(bf16), spread), 0.0)
    codes = jnp.sum(codes.reshape(NGROUPS, GROUP, 256), axis=1).astype(i32)
    rl = codes - 1
    keys = (rl & 15) * 16 + (rl >> 4) * 8 + owner_of[:16]
    key_scr[...] = jnp.where((codes > 0) & (codes < 64), keys, -1)
    sub = iota((16, 256), 0)

    def gather(g, _):
        block = from_rows(recv_ref, g, OUT)
        key = key_scr[pl.ds(g, 1), :]
        perm = jnp.concatenate([one(sub == key - 16 * i) for i in range(16)], axis=0)
        rows = jnp.concatenate([slot_rows(block, PAIRS), jnp.zeros((64, 256), bf16)], axis=0)
        x = dot(perm, rows).astype(bf16)
        for l in range(16):
            x_ref[l, pl.ds(pl.multiple_of(g * 16, 16), 16), :] = x[l * 16 : (l + 1) * 16]
        return 0

    lax.fori_loop(0, NGROUPS, gather, 0, unroll=4)
    x_copy = pltpu.make_async_copy(x_ref, x_any, x_sem)
    x_copy.start()
    raw = slot_major(pltpu.roll(ext, 96, 1)) - 1.0
    cc = cc_ref[...]
    tr_ref[...] = jnp.where(raw > -0.5, raw - cc * jnp.floor((raw + 0.5) / cc), -1.0)
    stat_ref[...] = jnp.zeros((256, 128), f32)
    lab_copy.wait()
    lane, wide = iota((16, 128), 1), iota((16, 256), 1)
    widef = wide.astype(f32)

    def cluster(l, _):
        lab = lab_ref[l]
        score = dot(x_ref[l], lab, 1, 1)
        valid = wide < counts_ref[l]
        weights, hits = [], []
        for i in range(16):
            at = slice(16 * i, 16 * i + 16)
            s = score[at]
            masked = jnp.where(valid, s, -jnp.inf)
            top = jnp.max(masked, axis=1, keepdims=True)
            weight = jnp.exp(masked - top)
            target = jnp.sum(jnp.where(lane == l, tr_ref[at, :], 0.0), axis=1, keepdims=True)
            hit = widef == target
            stat = jnp.where(lane == l, top, stat_ref[at, :])
            stat = jnp.where(lane == l + 16, jnp.sum(weight, axis=1, keepdims=True), stat)
            found = jnp.sum(jnp.where(hit, s, 0.0), axis=1, keepdims=True)
            stat_ref[at, :] = jnp.where(lane == l + 32, found, stat)
            weights.append(weight.astype(bf16))
            hits.append(one(hit))
        part_scr[l] = dot(jnp.concatenate(weights, axis=0), lab).astype(bf16)
        pos_scr[l] = dot(jnp.concatenate(hits, axis=0), lab).astype(bf16)
        return 0

    lax.fori_loop(0, 16, cluster, 0, unroll=4)
    lane, own_row = iota((16, 128), 1), iota((16, 128), 0)
    own_sub = iota((16, 1), 0).astype(f32)
    wide = iota((16, 256), 1)
    home = ((wide & 7) * 32 + ((wide >> 3) & 1) * 16 + (wide >> 4)).astype(f32)
    last = iota((GROUP, 8, 128), 1) == 7

    def scatter(g, _):
        at = pl.ds(pl.multiple_of(g * 16, 16), 16)
        parts = jnp.concatenate([part_scr[l, at, :] for l in range(16)], axis=0)
        pos = jnp.concatenate([pos_scr[l, at, :] for l in range(16)], axis=0)
        codes = ext_scr[pl.ds(pl.multiple_of(g * 64, 64), 64), :]
        own, other = [], []
        for i in range(16):
            c = codes[8 * (i // 2) : 8 * (i // 2) + 8]
            c = jnp.concatenate([c, c], axis=0)
            c = jnp.where(lane == 16 * (i % 2) + own_row, c, 0.0)
            code = jnp.sum(c, axis=1, keepdims=True) + (32.0 * (i // 2) - 1.0)
            is_pos = code > 32.0 * (i // 2) + 50.0
            is_part = (code > 32.0 * (i // 2) - 0.5) & (code < 32.0 * (i // 2) + 50.0)
            own.append(one(home == jnp.where(is_part, code, -1.0)))
            other.append(one(home == jnp.where(is_pos, code - 64.0, -1.0)))
        rows = dot(jnp.concatenate(own, axis=0), parts) + dot(jnp.concatenate(other, axis=0), pos)
        hi, mid, lo = pieces_of(stat_ref[at, :])
        stat = hi + pltpu.roll(mid, 48, 1)
        stat = stat + jnp.where(lane >= 112, pltpu.roll(lo, 80, 1), jnp.where(lane >= 96, pltpu.roll(lo, 96, 1), 0.0))
        halves = []
        for r in range(2):
            half = rows[:, 128 * r : 128 * r + 128].reshape(GROUP, SLOTS, 128)
            mine = jnp.broadcast_to(stat[8 * r : 8 * r + 8][:, None, :], (GROUP, 8, 128))
            halves += [half[:, :24], jnp.where(last, mine, half[:, 24:])]
        out = jnp.concatenate(halves, axis=1).reshape(GROUP * BACK, 128).astype(bf16)
        send_ref[pl.ds(pl.multiple_of(g * GROUP * BACK, GROUP * BACK), GROUP * BACK), :] = out
        send_block(send_ref, send_any, out_sems, g, BACK).start()
        return 0

    lax.fori_loop(0, NGROUPS, scatter, 0, unroll=8)
    x_copy.wait()
    for g in range(NGROUPS):
        send_block(send_ref, send_any, out_sems, g, BACK).wait()


def ready_kernel(
    counts_ref, sid_ref, stat_ref, trc_ref, acc_ref, x_any, lab_any,
    mask_ref, acct_ref, top_ref, tr_ref, weight_any, x_ref, lab_ref, weight_ref, sems,
):
    copies = [pltpu.make_async_copy(x_any, x_ref, sems.at[0]), pltpu.make_async_copy(lab_any, lab_ref, sems.at[1])]
    for copy in copies:
        copy.start()
    for copy in copies:
        copy.wait()
    acct_ref[...] = jnp.concatenate([acc_ref[...], jnp.zeros((112, 256), f32)], axis=0).T
    top_ref[...] = stat_ref[...].T[:16]
    r256 = iota((256, 256), 0)
    tr_ref[...] = trc_ref[...].T[:16]
    cols = jnp.concatenate([sid_ref[...].astype(f32), jnp.zeros((104, 256), f32)], axis=0).T
    lane = iota((256, 256), 1).astype(f32)

    def step(n, _):
        slot = lane + (n * 256).astype(f32)
        mask = cols[:, 0:1] == slot
        for k in range(1, 8):
            mask = mask | (cols[:, k : k + 1] == slot)
        pos = jnp.where(cols[:, 16:17] == slot, -1.0, 0.0)
        mask_ref[n] = jnp.where(mask, 1.0, pos).astype(bf16)
        score = dot(lab_ref[n], x_ref[n], 1, 1)
        weight_ref[n] = jnp.where(r256 < counts_ref[n], jnp.exp(score - top_ref[pl.ds(n, 1), :]), 0.0)
        return 0

    lax.fori_loop(0, NGROUPS, step, 0)
    copy = pltpu.make_async_copy(weight_ref, weight_any, sems.at[0])
    copy.start()
    copy.wait()


def lse_kernel(recv_ref, sid_ref, loss_ref, send_ref, scale_ref, left_scr, right_scr):
    def take(g, _):
        block = from_rows(recv_ref, g, BACK)
        at = pl.ds(pl.multiple_of(g * 64, 64), 64)
        left_scr[at, :] = block[:, 24:32].reshape(64, 128)
        right_scr[at, :] = block[:, 56:64].reshape(64, 128)
        return 0

    lax.fori_loop(0, NGROUPS, take, 0, unroll=16)
    stats = [scr[pl.ds(7, 128, stride=8), :].T for scr in (left_scr, right_scr)]
    table = jnp.concatenate(stats, axis=0).astype(bf16)
    i128, i16, i32s = iota((128, 256), 0), iota((16, 256), 0), iota((32, 256), 0)
    sid = sid_ref[...]
    tops, sums, ohs = [], [], []
    target = jnp.zeros((1, 256), f32)
    for k in range(8):
        rl = sid[8 + k : 9 + k]
        oh = one(i128 == (sid[k : k + 1] >> 5))
        got = dot(table, oh)
        got = jnp.where((rl & 16) == 0, got[:128], got[128:])
        mine = i16 == (rl & 15)
        tops.append(total(jnp.where(mine, got[:16] + got[48:64] + got[96:112], 0.0)))
        sums.append(total(jnp.where(mine, got[16:32] + got[64:80], 0.0)))
        target = target + total(jnp.where(mine, got[32:48] + got[80:96] + got[112:], 0.0))
        ohs.append(oh)
    largest = tops[0]
    for k in range(1, 8):
        largest = jnp.maximum(largest, tops[k])
    norm = sums[0] * jnp.exp(tops[0] - largest)
    for k in range(1, 8):
        norm = norm + sums[k] * jnp.exp(tops[k] - largest)
    lse = largest + jnp.log(norm)
    loss_ref[...] = lse - target
    split = pieces_of(lse)
    outs = []
    for k in range(8):
        j, rl = sid[k : k + 1] & 31, sid[8 + k : 9 + k]
        w = [jnp.where(i32s == rl, p, 0.0) for p in split]
        w += [jnp.where(i32s == j, p, 0.0) for p in pieces_of(jnp.exp(tops[k] - lse))]
        outs.append(jnp.concatenate(w, axis=0).astype(bf16))
    out = dot(jnp.concatenate(outs, axis=1), jnp.concatenate(ohs, axis=1), 1, 1)
    out = jnp.concatenate([out[:32] + out[32:64] + out[64:96], out[96:128] + out[128:160] + out[160:]], axis=0)
    out = jnp.concatenate([out, jnp.zeros((64, 128), f32)], axis=0).T
    send_ref[...] = out
    scale_ref[...] = jnp.where(iota((128, 128), 1) < 32, pltpu.roll(out, 96, 1), 0.0)


def combine_kernel(recv_ref, mask_ref, scale_ref, out_ref, row_scr):
    r256, c256 = iota((128, 256), 0), iota((128, 256), 1)
    spread = one((r256 == (c256 & 31)) & (r256 < 32))
    wide = jnp.zeros((128, 256), f32)
    for piece in pieces_of(scale_ref[...]):
        wide = wide + dot(piece.astype(bf16), spread)
    wide = jnp.where((r256 & 7) == (c256 >> 5), wide, 0.0)
    row_scr[...] = jnp.sum(wide.reshape(NGROUPS, GROUP, 256), axis=1)

    def group(g, acc):
        rows = slot_rows(from_rows(recv_ref, g, BACK), SLOTS)
        scale = row_scr[pl.ds(g, 1), :]
        his, los = [], []
        for i in range(16):
            mask = mask_ref[g, 16 * i : 16 * i + 16, :].astype(f32)
            a = jnp.where(mask > 0.5, scale, mask)
            hi = a.astype(bf16)
            his.append(hi)
            los.append((a - hi.astype(f32)).astype(bf16))
        return acc + (dot(jnp.concatenate(his, axis=0), rows) + dot(jnp.concatenate(los, axis=0), rows))

    out_ref[...] = lax.fori_loop(0, NGROUPS, group, jnp.zeros((256, 256), f32), unroll=8).astype(bf16)


PART = 4


def table_kernel(
    lse_ref, top_ref, tr_ref, acct_ref, weight_any, x_any, lab_any, new_any, nacc_ref,
    weight_ref, x_ref, lab_ref, fac_scr, new_scr, out_scr, in_sems, out_sems,
):
    def inputs_of(p):
        at = pl.ds(p * PART, PART)
        pairs = [(weight_any, weight_ref), (x_any, x_ref), (lab_any, lab_ref)]
        return [pltpu.make_async_copy(a.at[at], b.at[at], in_sems.at[n, p]) for n, (a, b) in enumerate(pairs)]

    def output_of(p):
        at = pl.ds(p * PART, PART)
        return pltpu.make_async_copy(new_scr.at[at], new_any.at[at], out_sems.at[p])

    for p in range(16 // PART):
        for copy in inputs_of(p):
            copy.start()
    fac_scr[...] = jnp.exp(top_ref[...] - slot_major(lse_ref[...]).T[:16])
    out_scr[...] = jnp.zeros((256, 128), f32)
    rowf = iota((16, 256), 0).astype(f32)
    lane = iota((16, 128), 1)

    def part(p, _):
        for copy in inputs_of(p):
            copy.wait()
        for q in range(PART):
            l = p * PART + q
            fac = fac_scr[pl.ds(l, 1), :]
            target = tr_ref[pl.ds(l, 1), :]
            strips = []
            for i in range(16):
                hit = rowf == target - 16.0 * i
                strips.append((weight_ref[l, 16 * i : 16 * i + 16, :] * fac - jnp.where(hit, 1.0, 0.0)).astype(bf16))
            grad = dot(jnp.concatenate(strips, axis=0), x_ref[l])
            for i in range(16):
                at = slice(16 * i, 16 * i + 16)
                g = grad[at]
                square = g * g
                both = (square[:, :128] + square[:, 128:]) * (1.0 / 256.0)
                both = both + jnp.where(lane == l, acct_ref[at, :], 0.0)
                accum = jnp.sum(both, axis=1, keepdims=True)
                new_scr[l, at, :] = lab_ref[l, at, :].astype(f32) - g * (STEP_RATE / jnp.sqrt(accum))
                out_scr[at, :] = jnp.where(lane == l, accum, out_scr[at, :])
        output_of(p).start()
        return 0

    lax.fori_loop(0, 16 // PART, part, 0)
    nacc_ref[...] = out_scr[...].T[:16]
    for p in range(16 // PART):
        output_of(p).wait()


def params(mib):
    return pltpu.CompilerParams(vmem_limit_bytes=mib * 1024 * 1024)


def shape(*dims, dtype=f32):
    return jax.ShapeDtypeStruct(dims, dtype)


VMEM = pl.BlockSpec(memory_space=pltpu.VMEM)
SMEM = pl.BlockSpec(memory_space=pltpu.SMEM)
HBM = pl.BlockSpec(memory_space=pltpu.HBM)


def in_hbm(x):
    return pltpu.with_memory_space_constraint(x, pltpu.HBM)


def exchange(x):
    return lax.all_to_all(x, "shard", split_axis=0, concat_axis=0, tiled=True)


def ranks_of(keys):
    order = jnp.argsort(keys, stable=True)
    sorted_keys = keys[order]
    places = jnp.arange(keys.shape[0], dtype=jnp.int32)
    starts = jnp.where((places == 0) | (sorted_keys != jnp.roll(sorted_keys, 1)), places, 0)
    starts = lax.cummax(starts)
    return jnp.zeros_like(keys).at[order].set(places - starts)


def scoring(recv_q, labels):
    return jnp.einsum("csw,clw->csl", recv_q, labels, preferred_element_type=jnp.float32)


def owner_share(score, top, valid, labels):
    weight = jnp.where(valid, jnp.exp(score - top[..., None]), 0.0).astype(jnp.bfloat16)
    return jnp.einsum("csl,clw->csw", weight, labels, preferred_element_type=jnp.float32).astype(
        jnp.bfloat16
    )


def send_back(share, pos_rows, devices):
    local_blocks, slot_rows, width = share.shape
    shaped = (local_blocks, devices, slot_rows // devices, width)
    return (
        lax.all_to_all(share.reshape(shaped), "shard", split_axis=1, concat_axis=1, tiled=True),
        lax.all_to_all(pos_rows.reshape(shaped), "shard", split_axis=1, concat_axis=1, tiled=True),
    )


def general(queries, clusters, placement, pos_pick, pos_row, counts, labels, accum):
    devices = lax.axis_size("shard")
    rows_dev, width = queries.shape
    per_query = clusters.shape[1]
    local_blocks, block_rows, _ = labels.shape
    most_rows = max(2, 2 * rows_dev * per_query // (local_blocks * devices))
    all_slots = local_blocks * devices * most_rows
    slot_rows = devices * most_rows
    flat = clusters.reshape(-1)
    rank = ranks_of(flat)
    block_ids = placement[flat]
    dest = block_ids // local_blocks
    local_id = block_ids % local_blocks
    where_to = (local_id * devices + dest) * most_rows + rank
    picked = jnp.arange(per_query, dtype=jnp.int32)[None, :] == pos_pick[:, None]
    target = jnp.where(picked, pos_row[:, None], -1).reshape(-1)
    send_q = (
        jnp.zeros((all_slots, width), jnp.bfloat16)
        .at[where_to]
        .set(jnp.repeat(queries, per_query, axis=0))
    )
    send_t = jnp.full((all_slots,), -1, jnp.int32).at[where_to].set(target)
    recv_q, recv_t = (
        lax.all_to_all(
            send_q.reshape(local_blocks, devices, most_rows, width),
            "shard",
            split_axis=1,
            concat_axis=1,
            tiled=True,
        ),
        lax.all_to_all(
            send_t.reshape(local_blocks, devices, most_rows),
            "shard",
            split_axis=1,
            concat_axis=1,
            tiled=True,
        ),
    )
    recv_q = recv_q.reshape(local_blocks, slot_rows, width)
    recv_t = recv_t.reshape(local_blocks, slot_rows)
    row_ids = jnp.arange(block_rows, dtype=jnp.int32)
    valid = row_ids[None, None, :] < counts[:, None, None]
    target_row = jnp.where(recv_t >= 0, recv_t % counts[:, None], -1)
    hit = row_ids[None, None, :] == target_row[..., None]
    score = scoring(recv_q, labels)
    masked = jnp.where(valid, score, -jnp.inf)
    top = jnp.max(masked, axis=-1)
    total = jnp.sum(jnp.exp(masked - top[..., None]), axis=-1)
    spos = jnp.sum(jnp.where(hit, score, 0.0), axis=-1)
    pos_rows = jnp.einsum(
        "csl,clw->csw", hit.astype(jnp.bfloat16), labels, preferred_element_type=jnp.float32
    ).astype(jnp.bfloat16)
    stat_shape = (local_blocks, devices, most_rows)
    back_m, back_z, back_s = (
        lax.all_to_all(top.reshape(stat_shape), "shard", split_axis=1, concat_axis=1, tiled=True),
        lax.all_to_all(total.reshape(stat_shape), "shard", split_axis=1, concat_axis=1, tiled=True),
        lax.all_to_all(spos.reshape(stat_shape), "shard", split_axis=1, concat_axis=1, tiled=True),
    )
    pair_m = back_m.reshape(-1)[where_to].reshape(rows_dev, per_query)
    pair_z = back_z.reshape(-1)[where_to].reshape(rows_dev, per_query)
    pair_s = back_s.reshape(-1)[where_to].reshape(rows_dev, per_query)
    largest = jnp.max(pair_m, axis=1)
    norm = jnp.sum(pair_z * jnp.exp(pair_m - largest[:, None]), axis=1)
    lse = largest + jnp.log(norm)
    loss = lse - jnp.sum(pair_s, axis=1)
    send_l = jnp.zeros((all_slots,), jnp.float32).at[where_to].set(jnp.repeat(lse, per_query))
    recv_l = lax.all_to_all(
        send_l.reshape(stat_shape), "shard", split_axis=1, concat_axis=1, tiled=True
    ).reshape(local_blocks, slot_rows)
    prob = jnp.where(valid, jnp.exp(score - recv_l[..., None]), 0.0)
    dlogit = (prob - hit.astype(jnp.float32)).astype(jnp.bfloat16)
    label_grad = jnp.einsum("csl,csw->clw", dlogit, recv_q, preferred_element_type=jnp.float32)
    returned, returned_pos = send_back(owner_share(score, top, valid, labels), pos_rows, devices)
    pieces = (
        returned.reshape(all_slots, width)[where_to]
        .astype(jnp.float32)
        .reshape(rows_dev, per_query, width)
    )
    pos_pieces = (
        returned_pos.reshape(all_slots, width)[where_to]
        .astype(jnp.float32)
        .reshape(rows_dev, per_query, width)
    )
    scale = jnp.exp(pair_m - lse[:, None])
    query_grad = (jnp.sum(pieces * scale[..., None], axis=1) - jnp.sum(pos_pieces, axis=1)).astype(
        jnp.bfloat16
    )
    new_accum = accum + jnp.mean(label_grad * label_grad, axis=-1)
    new_labels = (
        labels.astype(jnp.float32) - STEP_RATE * label_grad / jnp.sqrt(new_accum)[..., None]
    )
    return (new_labels, new_accum, query_grad, loss)


def shards(queries, clusters, placement, pos_pick, pos_row, counts, labels, accum):
    send, sid = pl.pallas_call(
        route_kernel,
        out_shape=(pltpu.HBM((DEVS * OUT, 128), bf16), pltpu.VMEM((24, 256), i32)),
        in_specs=[HBM] * 5,
        out_specs=(HBM, VMEM),
        scratch_shapes=[
            pltpu.VMEM((8, 256), i32),
            pltpu.VMEM((16, 128), i32),
            pltpu.VMEM((1, 256), i32),
            pltpu.VMEM((1, 256), i32),
            pltpu.VMEM((256, 256), bf16),
            pltpu.VMEM((DEVS * OUT, 128), bf16),
            pltpu.VMEM((128, 128), f32),
            pltpu.SemaphoreType.DMA((5,)),
            pltpu.SemaphoreType.DMA((NGROUPS,)),
        ],
        compiler_params=params(16),
        name="route",
    )(
        in_hbm(clusters.T), in_hbm(placement.reshape(16, 128)), in_hbm(pos_pick.reshape(1, 256)),
        in_hbm(pos_row.reshape(1, 256)), in_hbm(queries),
    )
    recv = exchange(send)
    lanes = jnp.concatenate([counts.astype(f32), jnp.ones((112,), f32)]).reshape(1, 128)
    x, slot_target, flag, stat, send = pl.pallas_call(
        owner_kernel,
        out_shape=(
            pltpu.HBM((16, 256, 256), bf16), pltpu.VMEM((256, 128), f32), shape(1, 1), pltpu.VMEM((256, 128), f32),
            pltpu.HBM((DEVS * BACK, 128), bf16),
        ),
        in_specs=[SMEM, VMEM, VMEM, HBM],
        out_specs=(HBM, VMEM, SMEM, VMEM, HBM),
        scratch_shapes=[
            pltpu.VMEM((16, 256, 256), bf16),
            pltpu.VMEM((16, 256, 256), bf16),
            pltpu.VMEM((DEVS * BACK, 128), bf16),
            pltpu.VMEM((1024, 128), f32),
            pltpu.VMEM((16, 256), i32),
            pltpu.VMEM((16, 256, 256), bf16),
            pltpu.VMEM((16, 256, 256), bf16),
            pltpu.SemaphoreType.DMA,
            pltpu.SemaphoreType.DMA,
            pltpu.SemaphoreType.DMA((NGROUPS,)),
        ],
        compiler_params=params(24),
        name="owner",
    )(counts, lanes, recv, in_hbm(labels))

    def plain():
        return general(queries, clusters, placement, pos_pick, pos_row, counts, labels, accum)

    def packed():
        return finish(counts, labels, accum, sid, x, slot_target, stat, send)

    return lax.cond(flag[0, 0] > 0.5, plain, packed)


def finish(counts, labels, accum, sid, x, slot_target, stat, send):
    recv = exchange(send)
    mask, acct, top, target, weight = pl.pallas_call(
        ready_kernel,
        out_shape=(
            pltpu.VMEM((NGROUPS, 256, 256), bf16), pltpu.VMEM((256, 128), f32), pltpu.VMEM((16, 256), f32),
            pltpu.VMEM((16, 256), f32), pltpu.HBM((16, 256, 256), f32),
        ),
        in_specs=[SMEM] + [VMEM] * 4 + [HBM] * 2,
        out_specs=(VMEM,) * 4 + (HBM,),
        scratch_shapes=[
            pltpu.VMEM((16, 256, 256), bf16),
            pltpu.VMEM((16, 256, 256), bf16),
            pltpu.VMEM((16, 256, 256), f32),
            pltpu.SemaphoreType.DMA((2,)),
        ],
        compiler_params=params(16),
        cost_estimate=pl.CostEstimate(flops=2 * 16 * 256**3, bytes_accessed=10_000_000, transcendentals=16 * 256**2),
        name="ready",
    )(counts, sid, stat, slot_target, accum, in_hbm(x), in_hbm(labels))
    loss, send, scale = pl.pallas_call(
        lse_kernel,
        out_shape=(shape(1, 256), shape(DEVS, 128), shape(DEVS, 128)),
        in_specs=[VMEM, VMEM],
        out_specs=(VMEM,) * 3,
        scratch_shapes=[pltpu.VMEM((1024, 128), f32)] * 2,
        compiler_params=params(8),
        name="normalizer",
    )(recv, sid)
    back = exchange(send)
    query_grad = pl.pallas_call(
        combine_kernel,
        out_shape=shape(256, 256, dtype=bf16),
        in_specs=[VMEM] * 3,
        out_specs=VMEM,
        scratch_shapes=[
            pltpu.VMEM((NGROUPS, 256), f32),
        ],
        compiler_params=params(8),
        cost_estimate=pl.CostEstimate(flops=2 * 2 * 256 * 4096 * 256, bytes_accessed=5_000_000, transcendentals=256 * 4096),
        name="combine",
    )(recv, mask, scale)
    new_labels, new_accum = pl.pallas_call(
        table_kernel,
        out_shape=(pltpu.HBM((16, 256, 256), f32), shape(16, 256)),
        in_specs=[VMEM] * 4 + [HBM] * 3,
        out_specs=(HBM, VMEM),
        scratch_shapes=[
            pltpu.VMEM((16, 256, 256), f32),
            pltpu.VMEM((16, 256, 256), bf16),
            pltpu.VMEM((16, 256, 256), bf16),
            pltpu.VMEM((16, 256), f32),
            pltpu.VMEM((16, 256, 256), f32),
            pltpu.VMEM((256, 128), f32),
            pltpu.SemaphoreType.DMA((3, 16 // PART)),
            pltpu.SemaphoreType.DMA((16 // PART,)),
        ],
        compiler_params=params(24),
        name="table",
    )(back, top, target, acct, in_hbm(weight), in_hbm(x), in_hbm(labels))

    return (new_labels, new_accum, query_grad, loss.reshape(256))


def solution(mesh):
    return jax.shard_map(
        shards,
        mesh=mesh,
        in_specs=(
            P("shard", None), P("shard", None), P(), P("shard"), P("shard"), P("shard"),
            P("shard", None, None), P("shard", None),
        ),
        out_specs=(P("shard", None, None), P("shard", None), P("shard", None), P("shard")),
        check_vma=False,
    )
```

time: 124 us -> 115 us (0.927)
  waiting for transfers between devices: 55.8 us -> 48.9 us
  Pallas kernels: 42.5 us -> 39.6 us
    all_to_all x3, waiting for transfers between devices: 55.8 us -> 48.9 us  [exchange(): return lax.all_to_all(x, 'shard', split_axis=0, concat_axis=0, tiled=True)]
    pallas_call x5, Pallas kernels: 32.4 us -> 29.4 us  [the longest x1 14 us: finish(): pl.pallas_call(ready_kernel, out_shape=(pltpu.VMEM((NGROUPS, 256, 256), b...]
    cond x0 -> x4, local copies, waits for them, and re-layouts: none -> 2.9 us
    unnamed x8 -> x18, local copies, waits for them, and re-layouts: 2.95 us -> 0.69 us
where the time goes in v2:
time: 115 us; the launch traced here: 114 us
  waiting for transfers between devices  48.9 us (43%)
  Pallas kernels  39.6 us (34%)
  starting transfers between devices  20.6 us (18%)
  local copies, waits for them, and re-layouts  3.59 us (3%)
  between operations  1.45 us (1%)
    all_to_all x3, waiting for transfers between devices, exchange(): return lax.all_to_all(x, 'shard', split_axis=0, concat_axis=0, tiled=True)  48.9 us
    all_to_all x3, starting transfers between devices, exchange(): return lax.all_to_all(x, 'shard', split_axis=0, concat_axis=0, tiled=True)  20.6 us
    pallas_call x1, Pallas kernels, finish(): pl.pallas_call(ready_kernel, out_shape=(pltpu.VMEM((NGROUPS, 256, 256), b...  14 us
    pallas_call x1, Pallas kernels, shards(): pl.pallas_call(owner_kernel, out_shape=(pltpu.HBM((16, 256, 256), bf16),...  10.1 us
    pallas_call x1, Pallas kernels, shards(): pl.pallas_call(route_kernel, out_shape=(pltpu.HBM((DEVS * OUT, 128), bf16...  6.01 us
    pallas_call x1, Pallas kernels, finish(): pl.pallas_call(table_kernel, out_shape=(pltpu.HBM((16, 256, 256), f32), s...  5.67 us
    cond x4, local copies, waits for them, and re-layouts  2.9 us
  transfers between devices with their start and end apart: 3, of which 3 were waited for; matrix products, arithmetic and copies ran while one was open for 0% of the time, Pallas kernels for 14%

profile of v2, /device:TPU:1, one launch (start us, length us, event | category | flops | bytes accessed | tf_op | source)
XLA Modules:
  0.0 114.4 jit_solution(15144259111105543606)
XLA Ops:
  0.6 0.0 copy-start.25
  0.6 6.0 %route.1 = (bf16[7168,128]{1,0:T(8,128)(2,1)}, s32[24,256]{1,0:T(8,128)S(1)}) custom-call(s32[8,256]{1,0:T(8,128)} %bitcast.53, s32[16,128]{1,0:T(8,128)} %bitcast.47, s32[1,256]{1,0:T(1,128)} %bitcast.55, s32[1,256]{1,0:T(1,128)} %bitcast.56, bf16[256,256]{1,0:T(8,128)(2,1)} %q_any.1), custom_call_target="tpu_custom_call" | custom-call | tf_op jit(solution)/shard_map/route/pallas_call | solution.py:578
  6.7 11.5 %all-to-all-start.10 = ((bf16[128,56,128]{2,1,0:T(8,128)(2,1)}), bf16[128,56,128]{2,1,0:T(8,128)(2,1)S(1)}, u32[]{:S(2)}, u32[]{:S(2)}) async-start(bf16[128,56,128]{2,1,0:T(8,128)(2,1)} %bitcast.49), calls=%async_computation.10 | async-start | bytes 3670016 | tf_op jit(solution)/shard_map/all_to_all | solution.py:451
  18.2 0.0 copy-done.25
  18.2 0.0 copy-start.2
  18.2 0.0 copy-start.6
  18.2 0.0 copy-start.18
  18.2 0.0 copy-start.21
  18.2 0.0 copy-start.26
  18.2 0.0 copy-start.27
  18.3 27.4 %all-to-all-done.10 = bf16[128,56,128]{2,1,0:T(8,128)(2,1)S(1)} async-done(((bf16[128,56,128]{2,1,0:T(8,128)(2,1)}), bf16[128,56,128]{2,1,0:T(8,128)(2,1)S(1)}, u32[]{:S(2)}, u32[]{:S(2)}) %all-to-all-start.10) | async-done | bytes 1835040 | tf_op jit(solution)/shard_map/all_to_all | solution.py:451
  45.7 10.1 %owner.1 = (bf16[16,256,256]{2,1,0:T(8,128)(2,1)}, f32[256,128]{1,0:T(8,128)S(1)}, f32[1,1]{1,0:T(1,128)}, f32[256,128]{1,0:T(8,128)S(1)}, bf16[8192,128]{1,0:T(8,128)(2,1)}) custom-call(s32[16]{0:T(128)S(1)} %copy-done.25, f32[1,128]{1,0:T(1,128)S(1)} %pad_bitcast_fusion.cc_ref, bf16[7168,128]{1,0:T(8,128)(2,1)S(1)} %bitcast.45, bf16[16,256,256]{2,1,0:T(8,128)(2,1)} %lab_any.1), custom_call_target="tpu_custom_call" | custom-call | tf_op jit(solution)/shard_map/owner/pallas_call | solution.py:602
  56.5 0.0 copy-done.2
  56.5 0.0 copy-done.6
  56.5 0.0 copy-done.18
  56.5 0.0 copy-done.21
  56.5 0.0 copy-done.26
  56.5 0.0 copy-done.27
  56.5 57.2 %conditional.1 = (f32[16,256]{1,0:T(8,128)S(1)}, bf16[256,256]{1,0:T(8,128)(2,1)S(1)}, f32[256]{0:T(256)}, f32[16,256,256]{2,1,0:T(8,128)}) conditional(s32[]{:T(128)} %bitcast.24, (bf16[8192,128]{1,0:T(8,128)(2,1)}, s32[24,256]{1,0:T(8,128)S(1)}, s32[16]{0:T(128)S(1)}, f32[256,128]{1,0:T(8,128)S(1)}, f32[256,128]{1,0:T(8,128)S(1)}, ...), branch_computations={%region_0.0_spmd, %region_1.18_spmd} | conditional | flops 2177789952 | bytes 174566560 | solution.py:632
  56.6 4.6 %all-to-all-start = ((bf16[128,64,128]{2,1,0:T(8,128)(2,1)}), bf16[128,64,128]{2,1,0:T(8,128)(2,1)S(1)}, u32[]{:S(2)}, u32[]{:S(2)}) async-start(bf16[128,64,128]{2,1,0:T(8,128)(2,1)} %bitcast.48), calls=%async_computation | async-start | bytes 4194304 | tf_op jit(solution)/shard_map/cond/branch_0_fun/all_to_all | solution.py:451
  61.2 14.0 %ready.1 = (bf16[16,256,256]{2,1,0:T(8,128)(2,1)S(1)}, f32[256,128]{1,0:T(8,128)S(1)}, f32[16,256]{1,0:T(8,128)S(1)}, f32[16,256]{1,0:T(8,128)S(1)}, f32[16,256,256]{2,1,0:T(8,128)}) custom-call(s32[16]{0:T(128)S(1)} %get-tuple-element.35.counts_ref, s32[24,256]{1,0:T(8,128)S(1)} %get-tuple-element.33.sid_ref, f32[256,128]{1,0:T(8,128)S(1)} %get-tuple-element.36.stat_ref, ...), custom_call_target="tpu_custom_call" | custom-call | flops 536870912 | bytes 10000000 | tf_op jit(solution)/shard_map/cond/branch_0_fun/ready/pallas_call | solution.py:637
  75.1 0.0 copy-start
  75.1 1.3 %copy-done = bf16[16,256,256]{2,1,0:T(8,128)(2,1)} copy-done((bf16[16,256,256]{2,1,0:T(8,128)(2,1)}, bf16[16,256,256]{2,1,0:T(8,128)(2,1)S(1)}, u32[]{:S(2)}) %copy-start) | copy-done | bytes 2097176 | tf_op jit(solution)/shard_map/cond
  76.5 15.2 %all-to-all-done = bf16[128,64,128]{2,1,0:T(8,128)(2,1)S(1)} async-done(((bf16[128,64,128]{2,1,0:T(8,128)(2,1)}), bf16[128,64,128]{2,1,0:T(8,128)(2,1)S(1)}, u32[]{:S(2)}, u32[]{:S(2)}) %all-to-all-start) | async-done | bytes 2097184 | tf_op jit(solution)/shard_map/cond/branch_0_fun/all_to_all | solution.py:451
  91.7 2.1 %normalizer.1 = (f32[1,256]{1,0:T(1,128)}, f32[128,128]{1,0:T(8,128)}, f32[128,128]{1,0:T(8,128)S(1)}) custom-call(bf16[8192,128]{1,0:T(8,128)(2,1)S(1)} %bitcast.43, s32[24,256]{1,0:T(8,128)S(1)} %get-tuple-element.33.sid_ref), custom_call_target="tpu_custom_call" | custom-call | tf_op jit(solution)/shard_map/cond/branch_0_fun/normalizer/pallas_call | solution.py:655
  93.8 4.5 %all-to-all-start.1 = ((f32[128,1,128]{2,1,0:T(1,128)}), f32[128,1,128]{2,1,0:T(1,128)S(1)}, u32[]{:S(2)}, u32[]{:S(2)}) async-start(f32[128,1,128]{2,1,0:T(1,128)} %bitcast.3), calls=%async_computation.1 | async-start | bytes 131072 | tf_op jit(solution)/shard_map/cond/branch_0_fun/all_to_all | solution.py:451
  98.3 0.0 copy-start.1
  98.3 1.6 %copy-done.1 = bf16[16,256,256]{2,1,0:T(8,128)(2,1)S(1)} copy-done((bf16[16,256,256]{2,1,0:T(8,128)(2,1)S(1)}, bf16[16,256,256]{2,1,0:T(8,128)(2,1)}, u32[]{:S(2)}) %copy-start.1) | copy-done | bytes 2097176 | tf_op jit(solution)/shard_map/cond
  99.9 1.7 %combine.1 = bf16[256,256]{1,0:T(8,128)(2,1)S(1)} custom-call(bf16[8192,128]{1,0:T(8,128)(2,1)S(1)} %bitcast.44, bf16[16,256,256]{2,1,0:T(8,128)(2,1)S(1)} %copy-done.1, f32[128,128]{1,0:T(8,128)S(1)} %get-tuple-element.48.scale_ref), custom_call_target="tpu_custom_call" | custom-call | flops 1073741824 | bytes 5000000 | tf_op jit(solution)/shard_map/cond/branch_0_fun/combine/pallas_call | solution.py:665
  101.6 6.2 %all-to-all-done.1 = f32[128,1,128]{2,1,0:T(1,128)S(1)} async-done(((f32[128,1,128]{2,1,0:T(1,128)}), f32[128,1,128]{2,1,0:T(1,128)S(1)}, u32[]{:S(2)}, u32[]{:S(2)}) %all-to-all-start.1) | async-done | bytes 65568 | tf_op jit(solution)/shard_map/cond/branch_0_fun/all_to_all | solution.py:451
  107.8 5.7 %table.1 = (f32[16,256,256]{2,1,0:T(8,128)}, f32[16,256]{1,0:T(8,128)S(1)}) custom-call(f32[128,128]{1,0:T(8,128)S(1)} %bitcast.46, f32[16,256]{1,0:T(8,128)S(1)} %get-tuple-element.41.top_ref, f32[16,256]{1,0:T(8,128)S(1)} %get-tuple-element.42.tr_ref, f32[256,128]{1,0:T(8,128)S(1)} %get-tuple-element.43.acct_ref, ...), custom_call_target="tpu_custom_call" | custom-call | tf_op jit(solution)/shard_map/cond/branch_0_fun/table/pallas_call | solution.py:677
  113.7 0.0 copy-start.13
  113.8 0.0 copy-start.29
  113.8 0.6 copy-done.13
  114.4 0.0 copy-done.29
  (2 shorter events, 0.0 us)
Async XLA Ops:
  0.6 17.5 %copy-start.25 = (s32[16]{0:T(128)S(1)}, s32[16]{0:T(128)}, u32[]{:S(2)}) copy-start(s32[16]{0:T(128)} %counts_ref.1) | copy-start | bytes 196
  6.7 39.0 %all-to-all-start.10 = ((bf16[128,56,128]{2,1,0:T(8,128)(2,1)}), bf16[128,56,128]{2,1,0:T(8,128)(2,1)S(1)}, u32[]{:S(2)}, u32[]{:S(2)}) async-start(bf16[128,56,128]{2,1,0:T(8,128)(2,1)} %bitcast.49), calls=%async_computation.10 | async-start | bytes 3670016 | tf_op jit(solution)/shard_map/all_to_all | solution.py:451
  18.2 38.3 %copy-start.2 = (s32[2048]{0:T(1024)S(1)}, s32[2048]{0:T(1024)}, u32[]{:S(2)}) copy-start(s32[2048]{0:T(1024)} %param.12) | copy-start | bytes 24580
  18.2 38.3 %copy-start.6 = (bf16[256,256]{1,0:T(8,128)(2,1)S(1)}, bf16[256,256]{1,0:T(8,128)(2,1)}, u32[]{:S(2)}) copy-start(bf16[256,256]{1,0:T(8,128)(2,1)} %q_any.1) | copy-start | bytes 393220
  18.2 38.3 %copy-start.18 = (f32[16,256]{1,0:T(8,128)S(1)}, f32[16,256]{1,0:T(8,128)}, u32[]{:S(2)}) copy-start(f32[16,256]{1,0:T(8,128)} %param.17) | copy-start | bytes 49156
  18.2 38.3 %copy-start.21 = (s32[256,8]{0,1:T(8,128)S(1)}, s32[256,8]{0,1:T(8,128)}, u32[]{:S(2)}) copy-start(s32[256,8]{0,1:T(8,128)} %param.11) | copy-start | bytes 24580
  18.2 38.3 %copy-start.26 = (s32[256]{0:T(256)S(1)}, s32[256]{0:T(256)}, u32[]{:S(2)}) copy-start(s32[256]{0:T(256)} %param.13) | copy-start | bytes 3076
  18.2 38.3 %copy-start.27 = (s32[256]{0:T(256)S(1)}, s32[256]{0:T(256)}, u32[]{:S(2)}) copy-start(s32[256]{0:T(256)} %param.14) | copy-start | bytes 3076
  56.6 35.1 %all-to-all-start = ((bf16[128,64,128]{2,1,0:T(8,128)(2,1)}), bf16[128,64,128]{2,1,0:T(8,128)(2,1)S(1)}, u32[]{:S(2)}, u32[]{:S(2)}) async-start(bf16[128,64,128]{2,1,0:T(8,128)(2,1)} %bitcast.48), calls=%async_computation | async-start | bytes 4194304 | tf_op jit(solution)/shard_map/cond/branch_0_fun/all_to_all | solution.py:451
  75.1 1.3 %copy-start = (bf16[16,256,256]{2,1,0:T(8,128)(2,1)}, bf16[16,256,256]{2,1,0:T(8,128)(2,1)S(1)}, u32[]{:S(2)}) copy-start(bf16[16,256,256]{2,1,0:T(8,128)(2,1)S(1)} %get-tuple-element.47.mask_ref) | copy-start | bytes 6291460 | tf_op jit(solution)/shard_map/cond
  93.8 14.1 %all-to-all-start.1 = ((f32[128,1,128]{2,1,0:T(1,128)}), f32[128,1,128]{2,1,0:T(1,128)S(1)}, u32[]{:S(2)}, u32[]{:S(2)}) async-start(f32[128,1,128]{2,1,0:T(1,128)} %bitcast.3), calls=%async_computation.1 | async-start | bytes 131072 | tf_op jit(solution)/shard_map/cond/branch_0_fun/all_to_all | solution.py:451
  98.3 1.6 %copy-start.1 = (bf16[16,256,256]{2,1,0:T(8,128)(2,1)S(1)}, bf16[16,256,256]{2,1,0:T(8,128)(2,1)}, u32[]{:S(2)}) copy-start(bf16[16,256,256]{2,1,0:T(8,128)(2,1)} %copy-done) | copy-start | bytes 6291460 | tf_op jit(solution)/shard_map/cond
  113.7 0.7 copy-start.13
  113.8 0.6 copy-start.29

commit v3 on v2

--- a/solution.py
+++ b/solution.py
@@ -221,16 +221,15 @@
             target = jnp.sum(jnp.where(lane == l, tr_ref[at, :], 0.0), axis=1, keepdims=True)
             hit = widef == target
             stat = jnp.where(lane == l, top, stat_ref[at, :])
-            stat = jnp.where(lane == l + 16, jnp.sum(weight, axis=1, keepdims=True), stat)
-            found = jnp.sum(jnp.where(hit, s, 0.0), axis=1, keepdims=True)
-            stat_ref[at, :] = jnp.where(lane == l + 32, found, stat)
+            stat_ref[at, :] = jnp.where(lane == l + 16, jnp.sum(weight, axis=1, keepdims=True), stat)
             weights.append(weight.astype(bf16))
             hits.append(one(hit))
-        part_scr[l] = dot(jnp.concatenate(weights, axis=0), lab).astype(bf16)
-        pos_scr[l] = dot(jnp.concatenate(hits, axis=0), lab).astype(bf16)
+        both = dot(jnp.concatenate(weights + hits, axis=0), lab)
+        part_scr[l] = both[:256].astype(bf16)
+        pos_scr[l] = both[256:].astype(bf16)
         return 0
 
-    lax.fori_loop(0, 16, cluster, 0, unroll=4)
+    lax.fori_loop(0, 16, cluster, 0, unroll=8)
     lane, own_row = iota((16, 128), 1), iota((16, 128), 0)
     own_sub = iota((16, 1), 0).astype(f32)
     wide = iota((16, 256), 1)
@@ -254,8 +253,7 @@
             other.append(one(home == jnp.where(is_pos, code - 64.0, -1.0)))
         rows = dot(jnp.concatenate(own, axis=0), parts) + dot(jnp.concatenate(other, axis=0), pos)
         hi, mid, lo = pieces_of(stat_ref[at, :])
-        stat = hi + pltpu.roll(mid, 48, 1)
-        stat = stat + jnp.where(lane >= 112, pltpu.roll(lo, 80, 1), jnp.where(lane >= 96, pltpu.roll(lo, 96, 1), 0.0))
+        stat = hi + pltpu.roll(mid, 32, 1) + pltpu.roll(lo, 64, 1)
         halves = []
         for r in range(2):
             half = rows[:, 128 * r : 128 * r + 128].reshape(GROUP, SLOTS, 128)
@@ -305,7 +303,7 @@
     copy.wait()
 
 
-def lse_kernel(recv_ref, sid_ref, loss_ref, send_ref, scale_ref, left_scr, right_scr):
+def lse_kernel(recv_ref, sid_ref, lse_ref, send_ref, scale_ref, left_scr, right_scr):
     def take(g, _):
         block = from_rows(recv_ref, g, BACK)
         at = pl.ds(pl.multiple_of(g * 64, 64), 64)
@@ -319,16 +317,14 @@
     i128, i16, i32s = iota((128, 256), 0), iota((16, 256), 0), iota((32, 256), 0)
     sid = sid_ref[...]
     tops, sums, ohs = [], [], []
-    target = jnp.zeros((1, 256), f32)
     for k in range(8):
         rl = sid[8 + k : 9 + k]
         oh = one(i128 == (sid[k : k + 1] >> 5))
         got = dot(table, oh)
         got = jnp.where((rl & 16) == 0, got[:128], got[128:])
         mine = i16 == (rl & 15)
-        tops.append(total(jnp.where(mine, got[:16] + got[48:64] + got[96:112], 0.0)))
-        sums.append(total(jnp.where(mine, got[16:32] + got[64:80], 0.0)))
-        target = target + total(jnp.where(mine, got[32:48] + got[80:96] + got[112:], 0.0))
+        tops.append(total(jnp.where(mine, got[:16] + got[32:48] + got[64:80], 0.0)))
+        sums.append(total(jnp.where(mine, got[16:32] + got[48:64] + got[80:96], 0.0)))
         ohs.append(oh)
     largest = tops[0]
     for k in range(1, 8):
@@ -337,7 +333,7 @@
     for k in range(1, 8):
         norm = norm + sums[k] * jnp.exp(tops[k] - largest)
     lse = largest + jnp.log(norm)
-    loss_ref[...] = lse - target
+    lse_ref[...] = lse
     split = pieces_of(lse)
     outs = []
     for k in range(8):
@@ -352,7 +348,7 @@
     scale_ref[...] = jnp.where(iota((128, 128), 1) < 32, pltpu.roll(out, 96, 1), 0.0)
 
 
-def combine_kernel(recv_ref, mask_ref, scale_ref, out_ref, row_scr):
+def combine_kernel(recv_ref, mask_ref, scale_ref, lse_ref, q_ref, out_ref, loss_ref, row_scr):
     r256, c256 = iota((128, 256), 0), iota((128, 256), 1)
     spread = one((r256 == (c256 & 31)) & (r256 < 32))
     wide = jnp.zeros((128, 256), f32)
@@ -361,27 +357,34 @@
     wide = jnp.where((r256 & 7) == (c256 >> 5), wide, 0.0)
     row_scr[...] = jnp.sum(wide.reshape(NGROUPS, GROUP, 256), axis=1)
 
-    def group(g, acc):
+    def group(g, accs):
+        acc, pos = accs
         rows = slot_rows(from_rows(recv_ref, g, BACK), SLOTS)
         scale = row_scr[pl.ds(g, 1), :]
-        his, los = [], []
+        his, los, places = [], [], []
         for i in range(16):
             mask = mask_ref[g, 16 * i : 16 * i + 16, :].astype(f32)
-            a = jnp.where(mask > 0.5, scale, mask)
+            a = jnp.where(mask > 0.5, scale, 0.0)
             hi = a.astype(bf16)
             his.append(hi)
             los.append((a - hi.astype(f32)).astype(bf16))
-        return acc + (dot(jnp.concatenate(his, axis=0), rows) + dot(jnp.concatenate(los, axis=0), rows))
-
-    out_ref[...] = lax.fori_loop(0, NGROUPS, group, jnp.zeros((256, 256), f32), unroll=8).astype(bf16)
+            places.append(one(mask < -0.5))
+        acc = acc + (dot(jnp.concatenate(his, axis=0), rows) + dot(jnp.concatenate(los, axis=0), rows))
+        return acc, pos + dot(jnp.concatenate(places, axis=0), rows)
+
+    zero = jnp.zeros((256, 256), f32)
+    acc, pos = lax.fori_loop(0, NGROUPS, group, (zero, zero), unroll=4)
+    out_ref[...] = (acc - pos).astype(bf16)
+    score = jnp.sum(q_ref[...].astype(f32) * pos, axis=1, keepdims=True)
+    loss_ref[...] = lse_ref[...] - jnp.broadcast_to(score, (256, 128)).T[:1]
 
 
 PART = 4
 
 
 def table_kernel(
-    lse_ref, top_ref, tr_ref, acct_ref, weight_any, x_any, lab_any, new_any, nacc_ref,
-    weight_ref, x_ref, lab_ref, fac_scr, new_scr, out_scr, in_sems, out_sems,
+    lse_ref, top_ref, tr_ref, acct_ref, weight_any, x_any, lab_any, new_any, nacc_any,
+    weight_ref, x_ref, lab_ref, fac_scr, new_scr, out_scr, nacc_ref, in_sems, out_sems, nacc_sem,
 ):
     def inputs_of(p):
         at = pl.ds(p * PART, PART)
@@ -426,6 +429,9 @@
 
     lax.fori_loop(0, 16 // PART, part, 0)
     nacc_ref[...] = out_scr[...].T[:16]
+    nacc_copy = pltpu.make_async_copy(nacc_ref, nacc_any, nacc_sem)
+    nacc_copy.start()
+    nacc_copy.wait()
     for p in range(16 // PART):
         output_of(p).wait()
 
@@ -627,12 +633,12 @@
         return general(queries, clusters, placement, pos_pick, pos_row, counts, labels, accum)
 
     def packed():
-        return finish(counts, labels, accum, sid, x, slot_target, stat, send)
+        return finish(queries, counts, labels, accum, sid, x, slot_target, stat, send)
 
     return lax.cond(flag[0, 0] > 0.5, plain, packed)
 
 
-def finish(counts, labels, accum, sid, x, slot_target, stat, send):
+def finish(queries, counts, labels, accum, sid, x, slot_target, stat, send):
     recv = exchange(send)
     mask, acct, top, target, weight = pl.pallas_call(
         ready_kernel,
@@ -652,7 +658,7 @@
         cost_estimate=pl.CostEstimate(flops=2 * 16 * 256**3, bytes_accessed=10_000_000, transcendentals=16 * 256**2),
         name="ready",
     )(counts, sid, stat, slot_target, accum, in_hbm(x), in_hbm(labels))
-    loss, send, scale = pl.pallas_call(
+    lse, send, scale = pl.pallas_call(
         lse_kernel,
         out_shape=(shape(1, 256), shape(DEVS, 128), shape(DEVS, 128)),
         in_specs=[VMEM, VMEM],
@@ -662,23 +668,23 @@
         name="normalizer",
     )(recv, sid)
     back = exchange(send)
-    query_grad = pl.pallas_call(
+    query_grad, loss = pl.pallas_call(
         combine_kernel,
-        out_shape=shape(256, 256, dtype=bf16),
-        in_specs=[VMEM] * 3,
-        out_specs=VMEM,
+        out_shape=(pltpu.HBM((256, 256), bf16), pltpu.HBM((1, 256), f32)),
+        in_specs=[VMEM] * 5,
+        out_specs=(VMEM, VMEM),
         scratch_shapes=[
             pltpu.VMEM((NGROUPS, 256), f32),
         ],
         compiler_params=params(8),
         cost_estimate=pl.CostEstimate(flops=2 * 2 * 256 * 4096 * 256, bytes_accessed=5_000_000, transcendentals=256 * 4096),
         name="combine",
-    )(recv, mask, scale)
+    )(recv, mask, scale, lse, queries)
     new_labels, new_accum = pl.pallas_call(
         table_kernel,
-        out_shape=(pltpu.HBM((16, 256, 256), f32), shape(16, 256)),
+        out_shape=(pltpu.HBM((16, 256, 256), f32), pltpu.HBM((16, 256), f32)),
         in_specs=[VMEM] * 4 + [HBM] * 3,
-        out_specs=(HBM, VMEM),
+        out_specs=(HBM, HBM),
         scratch_shapes=[
             pltpu.VMEM((16, 256, 256), f32),
             pltpu.VMEM((16, 256, 256), bf16),
@@ -686,8 +692,10 @@
             pltpu.VMEM((16, 256), f32),
             pltpu.VMEM((16, 256, 256), f32),
             pltpu.VMEM((256, 128), f32),
+            pltpu.VMEM((16, 256), f32),
             pltpu.SemaphoreType.DMA((3, 16 // PART)),
             pltpu.SemaphoreType.DMA((16 // PART,)),
+            pltpu.SemaphoreType.DMA,
         ],
         compiler_params=params(24),
         name="table",

time: 115 us -> 113 us (0.983)
  waiting for transfers between devices: 48.9 us -> 46.9 us
    pallas_call x2, Pallas kernels: 7.39 us -> 9.46 us  [the longest x1 5.7 us: finish(): pl.pallas_call(table_kernel, out_shape=(pltpu.HBM((16, 256, 256), f32), p...]
    all_to_all x3, waiting for transfers between devices: 48.9 us -> 46.9 us  [exchange(): return lax.all_to_all(x, 'shard', split_axis=0, concat_axis=0, tiled=True)]
    pallas_call x1, Pallas kernels: 10.1 us -> 8.99 us  [shards(): pl.pallas_call(owner_kernel, out_shape=(pltpu.HBM((16, 256, 256), bf16),...]
  transfers between devices with their start and end apart: 3 -> 3, of which waited for: 3 -> 3; matrix products, arithmetic and copies ran while one was open for 0% -> 0% of each run, Pallas kernels for 14% -> 16%
where the time goes in v3:
time: 113 us
  waiting for transfers between devices  46.9 us (42%)
  Pallas kernels  40.5 us (36%)
  starting transfers between devices  20.5 us (18%)
  local copies, waits for them, and re-layouts  2.95 us (3%)
  between operations  1.63 us (1%)
    all_to_all x3, waiting for transfers between devices, exchange(): return lax.all_to_all(x, 'shard', split_axis=0, concat_axis=0, tiled=True)  46.9 us
    all_to_all x3, starting transfers between devices, exchange(): return lax.all_to_all(x, 'shard', split_axis=0, concat_axis=0, tiled=True)  20.5 us
    pallas_call x1, Pallas kernels, finish(): pl.pallas_call(ready_kernel, out_shape=(pltpu.VMEM((NGROUPS, 256, 256), b...  13.9 us
    pallas_call x1, Pallas kernels, shards(): pl.pallas_call(owner_kernel, out_shape=(pltpu.HBM((16, 256, 256), bf16),...  8.99 us
    pallas_call x1, Pallas kernels, shards(): pl.pallas_call(route_kernel, out_shape=(pltpu.HBM((DEVS * OUT, 128), bf16...  6.01 us
    pallas_call x1, Pallas kernels, finish(): pl.pallas_call(table_kernel, out_shape=(pltpu.HBM((16, 256, 256), f32), p...  5.7 us
    pallas_call x1, Pallas kernels, finish(): pl.pallas_call(combine_kernel, out_shape=(pltpu.HBM((256, 256), bf16), pl...  3.76 us
    cond x4, local copies, waits for them, and re-layouts  2.9 us
  transfers between devices with their start and end apart: 3, of which 3 were waited for; matrix products, arithmetic and copies ran while one was open for 0% of the time, Pallas kernels for 16%

profile of v3, /device:TPU:1, one launch (start us, length us, event | category | flops | bytes accessed | tf_op | source)
XLA Modules:
  0.0 113.0 jit_solution(4103815727907201014)
XLA Ops:
  0.6 0.0 copy-start.24
  0.6 6.0 %route.1 = (bf16[7168,128]{1,0:T(8,128)(2,1)}, s32[24,256]{1,0:T(8,128)S(1)}) custom-call(s32[8,256]{1,0:T(8,128)} %bitcast.53, s32[16,128]{1,0:T(8,128)} %bitcast.47, s32[1,256]{1,0:T(1,128)} %bitcast.55, s32[1,256]{1,0:T(1,128)} %bitcast.56, bf16[256,256]{1,0:T(8,128)(2,1)} %q_any.1), custom_call_target="tpu_custom_call" | custom-call | tf_op jit(solution)/shard_map/route/pallas_call | solution.py:584
  6.7 11.5 %all-to-all-start.10 = ((bf16[128,56,128]{2,1,0:T(8,128)(2,1)}), bf16[128,56,128]{2,1,0:T(8,128)(2,1)S(1)}, u32[]{:S(2)}, u32[]{:S(2)}) async-start(bf16[128,56,128]{2,1,0:T(8,128)(2,1)} %bitcast.49), calls=%async_computation.10 | async-start | bytes 3670016 | tf_op jit(solution)/shard_map/all_to_all | solution.py:457
  18.2 0.0 copy-done.24
  18.2 0.0 copy-start.2
  18.2 0.0 copy-start.6
  18.2 0.0 copy-start.17
  18.2 0.0 copy-start.20
  18.2 0.0 copy-start.25
  18.2 0.0 copy-start.26
  18.3 27.4 %all-to-all-done.10 = bf16[128,56,128]{2,1,0:T(8,128)(2,1)S(1)} async-done(((bf16[128,56,128]{2,1,0:T(8,128)(2,1)}), bf16[128,56,128]{2,1,0:T(8,128)(2,1)S(1)}, u32[]{:S(2)}, u32[]{:S(2)}) %all-to-all-start.10) | async-done | bytes 1835040 | tf_op jit(solution)/shard_map/all_to_all | solution.py:457
  45.7 9.0 %owner.1 = (bf16[16,256,256]{2,1,0:T(8,128)(2,1)}, f32[256,128]{1,0:T(8,128)S(1)}, f32[1,1]{1,0:T(1,128)}, f32[256,128]{1,0:T(8,128)S(1)}, bf16[8192,128]{1,0:T(8,128)(2,1)}) custom-call(s32[16]{0:T(128)S(1)} %copy-done.24, f32[1,128]{1,0:T(1,128)S(1)} %pad_bitcast_fusion.cc_ref, bf16[7168,128]{1,0:T(8,128)(2,1)S(1)} %bitcast.45, bf16[16,256,256]{2,1,0:T(8,128)(2,1)} %lab_any.1), custom_call_target="tpu_custom_call" | custom-call | tf_op jit(solution)/shard_map/owner/pallas_call | solution.py:608
  55.3 0.0 copy-done.2
  55.3 0.0 copy-done.6
  55.3 0.0 copy-done.17
  55.4 0.0 copy-done.20
  55.4 0.0 copy-done.25
  55.4 0.0 copy-done.26
  55.4 57.4 %conditional.1 = (f32[16,256]{1,0:T(8,128)}, bf16[256,256]{1,0:T(8,128)(2,1)}, f32[256]{0:T(256)}, f32[16,256,256]{2,1,0:T(8,128)}) conditional(s32[]{:T(128)} %bitcast.24, (bf16[8192,128]{1,0:T(8,128)(2,1)}, s32[24,256]{1,0:T(8,128)S(1)}, s32[16]{0:T(128)S(1)}, f32[256,128]{1,0:T(8,128)S(1)}, f32[256,128]{1,0:T(8,128)S(1)}, ...), branch_computations={%region_0.0_spmd, %region_1.18_spmd} | conditional | flops 2177789952 | bytes 174500992 | solution.py:638
  55.4 4.6 %all-to-all-start = ((bf16[128,64,128]{2,1,0:T(8,128)(2,1)}), bf16[128,64,128]{2,1,0:T(8,128)(2,1)S(1)}, u32[]{:S(2)}, u32[]{:S(2)}) async-start(bf16[128,64,128]{2,1,0:T(8,128)(2,1)} %bitcast.48), calls=%async_computation | async-start | bytes 4194304 | tf_op jit(solution)/shard_map/cond/branch_0_fun/all_to_all | solution.py:457
  60.0 13.9 %ready.1 = (bf16[16,256,256]{2,1,0:T(8,128)(2,1)S(1)}, f32[256,128]{1,0:T(8,128)S(1)}, f32[16,256]{1,0:T(8,128)S(1)}, f32[16,256]{1,0:T(8,128)S(1)}, f32[16,256,256]{2,1,0:T(8,128)}) custom-call(s32[16]{0:T(128)S(1)} %get-tuple-element.37.counts_ref, s32[24,256]{1,0:T(8,128)S(1)} %get-tuple-element.35.sid_ref, f32[256,128]{1,0:T(8,128)S(1)} %get-tuple-element.38.stat_ref, ...), custom_call_target="tpu_custom_call" | custom-call | flops 536870912 | bytes 10000000 | tf_op jit(solution)/shard_map/cond/branch_0_fun/ready/pallas_call | solution.py:643
  74.0 0.0 copy-start
  74.0 1.3 %copy-done = bf16[16,256,256]{2,1,0:T(8,128)(2,1)} copy-done((bf16[16,256,256]{2,1,0:T(8,128)(2,1)}, bf16[16,256,256]{2,1,0:T(8,128)(2,1)S(1)}, u32[]{:S(2)}) %copy-start) | copy-done | bytes 2097176 | tf_op jit(solution)/shard_map/cond
  75.3 15.3 %all-to-all-done = bf16[128,64,128]{2,1,0:T(8,128)(2,1)S(1)} async-done(((bf16[128,64,128]{2,1,0:T(8,128)(2,1)}), bf16[128,64,128]{2,1,0:T(8,128)(2,1)S(1)}, u32[]{:S(2)}, u32[]{:S(2)}) %all-to-all-start) | async-done | bytes 2097184 | tf_op jit(solution)/shard_map/cond/branch_0_fun/all_to_all | solution.py:457
  90.5 2.1 %normalizer.1 = (f32[1,256]{1,0:T(1,128)S(1)}, f32[128,128]{1,0:T(8,128)}, f32[128,128]{1,0:T(8,128)S(1)}) custom-call(bf16[8192,128]{1,0:T(8,128)(2,1)S(1)} %bitcast.43, s32[24,256]{1,0:T(8,128)S(1)} %get-tuple-element.35.sid_ref), custom_call_target="tpu_custom_call" | custom-call | tf_op jit(solution)/shard_map/cond/branch_0_fun/normalizer/pallas_call | solution.py:661
  92.6 4.4 %all-to-all-start.1 = ((f32[128,1,128]{2,1,0:T(1,128)}), f32[128,1,128]{2,1,0:T(1,128)S(1)}, u32[]{:S(2)}, u32[]{:S(2)}) async-start(f32[128,1,128]{2,1,0:T(1,128)} %bitcast.3), calls=%async_computation.1 | async-start | bytes 131072 | tf_op jit(solution)/shard_map/cond/branch_0_fun/all_to_all | solution.py:457
  97.0 0.0 copy-start.1
  97.1 1.6 %copy-done.1 = bf16[16,256,256]{2,1,0:T(8,128)(2,1)S(1)} copy-done((bf16[16,256,256]{2,1,0:T(8,128)(2,1)S(1)}, bf16[16,256,256]{2,1,0:T(8,128)(2,1)}, u32[]{:S(2)}) %copy-start.1) | copy-done | bytes 2097176 | tf_op jit(solution)/shard_map/cond
  98.6 3.8 %combine.1 = (bf16[256,256]{1,0:T(8,128)(2,1)}, f32[1,256]{1,0:T(1,128)}) custom-call(bf16[8192,128]{1,0:T(8,128)(2,1)S(1)} %bitcast.44, bf16[16,256,256]{2,1,0:T(8,128)(2,1)S(1)} %copy-done.1, f32[128,128]{1,0:T(8,128)S(1)} %get-tuple-element.50.scale_ref, f32[1,256]{1,0:T(1,128)S(1)} %get-tuple-element.51.lse_ref, bf16[256,256]{1,0:T(8,128)(2,1)S(1)} %get-tuple-element.52.q_ref), custom_call_target="tpu_custom_call" | custom-call | flops 1073741824 | bytes 5000000 | tf_op jit(solution)/shard_map/cond/branch_0_fun/combine/pallas_call | solution.py:671
  102.4 4.3 %all-to-all-done.1 = f32[128,1,128]{2,1,0:T(1,128)S(1)} async-done(((f32[128,1,128]{2,1,0:T(1,128)}), f32[128,1,128]{2,1,0:T(1,128)S(1)}, u32[]{:S(2)}, u32[]{:S(2)}) %all-to-all-start.1) | async-done | bytes 65568 | tf_op jit(solution)/shard_map/cond/branch_0_fun/all_to_all | solution.py:457
  106.7 5.7 %table.1 = (f32[16,256,256]{2,1,0:T(8,128)}, f32[16,256]{1,0:T(8,128)}) custom-call(f32[128,128]{1,0:T(8,128)S(1)} %bitcast.46, f32[16,256]{1,0:T(8,128)S(1)} %get-tuple-element.43.top_ref, f32[16,256]{1,0:T(8,128)S(1)} %get-tuple-element.44.tr_ref, f32[256,128]{1,0:T(8,128)S(1)} %get-tuple-element.45.acct_ref, ...), custom_call_target="tpu_custom_call" | custom-call | tf_op jit(solution)/shard_map/cond/branch_0_fun/table/pallas_call | solution.py:683
  (2 shorter events, 0.0 us)
Async XLA Ops:
  0.6 17.5 %copy-start.24 = (s32[16]{0:T(128)S(1)}, s32[16]{0:T(128)}, u32[]{:S(2)}) copy-start(s32[16]{0:T(128)} %counts_ref.1) | copy-start | bytes 196
  6.7 39.0 %all-to-all-start.10 = ((bf16[128,56,128]{2,1,0:T(8,128)(2,1)}), bf16[128,56,128]{2,1,0:T(8,128)(2,1)S(1)}, u32[]{:S(2)}, u32[]{:S(2)}) async-start(bf16[128,56,128]{2,1,0:T(8,128)(2,1)} %bitcast.49), calls=%async_computation.10 | async-start | bytes 3670016 | tf_op jit(solution)/shard_map/all_to_all | solution.py:457
  18.2 37.2 %copy-start.2 = (s32[2048]{0:T(1024)S(1)}, s32[2048]{0:T(1024)}, u32[]{:S(2)}) copy-start(s32[2048]{0:T(1024)} %param.12) | copy-start | bytes 24580
  18.2 37.2 %copy-start.6 = (bf16[256,256]{1,0:T(8,128)(2,1)S(1)}, bf16[256,256]{1,0:T(8,128)(2,1)}, u32[]{:S(2)}) copy-start(bf16[256,256]{1,0:T(8,128)(2,1)} %q_any.1) | copy-start | bytes 393220
  18.2 37.2 %copy-start.17 = (f32[16,256]{1,0:T(8,128)S(1)}, f32[16,256]{1,0:T(8,128)}, u32[]{:S(2)}) copy-start(f32[16,256]{1,0:T(8,128)} %param.17) | copy-start | bytes 49156
  18.2 37.1 %copy-start.20 = (s32[256,8]{0,1:T(8,128)S(1)}, s32[256,8]{0,1:T(8,128)}, u32[]{:S(2)}) copy-start(s32[256,8]{0,1:T(8,128)} %param.11) | copy-start | bytes 24580
  18.2 37.1 %copy-start.25 = (s32[256]{0:T(256)S(1)}, s32[256]{0:T(256)}, u32[]{:S(2)}) copy-start(s32[256]{0:T(256)} %param.13) | copy-start | bytes 3076
  18.2 37.1 %copy-start.26 = (s32[256]{0:T(256)S(1)}, s32[256]{0:T(256)}, u32[]{:S(2)}) copy-start(s32[256]{0:T(256)} %param.14) | copy-start | bytes 3076
  55.4 35.1 %all-to-all-start = ((bf16[128,64,128]{2,1,0:T(8,128)(2,1)}), bf16[128,64,128]{2,1,0:T(8,128)(2,1)S(1)}, u32[]{:S(2)}, u32[]{:S(2)}) async-start(bf16[128,64,128]{2,1,0:T(8,128)(2,1)} %bitcast.48), calls=%async_computation | async-start | bytes 4194304 | tf_op jit(solution)/shard_map/cond/branch_0_fun/all_to_all | solution.py:457
  74.0 1.3 %copy-start = (bf16[16,256,256]{2,1,0:T(8,128)(2,1)}, bf16[16,256,256]{2,1,0:T(8,128)(2,1)S(1)}, u32[]{:S(2)}) copy-start(bf16[16,256,256]{2,1,0:T(8,128)(2,1)S(1)} %get-tuple-element.49.mask_ref) | copy-start | bytes 6291460 | tf_op jit(solution)/shard_map/cond
  92.6 14.1 %all-to-all-start.1 = ((f32[128,1,128]{2,1,0:T(1,128)}), f32[128,1,128]{2,1,0:T(1,128)S(1)}, u32[]{:S(2)}, u32[]{:S(2)}) async-start(f32[128,1,128]{2,1,0:T(1,128)} %bitcast.3), calls=%async_computation.1 | async-start | bytes 131072 | tf_op jit(solution)/shard_map/cond/branch_0_fun/all_to_all | solution.py:457
  97.0 1.6 %copy-start.1 = (bf16[16,256,256]{2,1,0:T(8,128)(2,1)S(1)}, bf16[16,256,256]{2,1,0:T(8,128)(2,1)}, u32[]{:S(2)}) copy-start(bf16[16,256,256]{2,1,0:T(8,128)(2,1)} %copy-done) | copy-start | bytes 6291460 | tf_op jit(solution)/shard_map/cond

commit v4 on v3

--- a/solution.py
+++ b/solution.py
@@ -24,6 +24,10 @@
 
 def one(mask):
     return jnp.where(mask, 1.0, 0.0).astype(bf16)
+
+
+def one16(mask):
+    return jnp.where(mask, jnp.ones((), bf16), jnp.zeros((), bf16))
 
 
 def dot(a, b, ca=1, cb=0):
@@ -124,20 +128,19 @@
     sid_ref[...] = jnp.concatenate(
         [d * SLOTS + j for d, j in zip(ds, js)] + rls + [dp * SLOTS + jp] + [jnp.zeros((1, 256), i32)] * 7, axis=0
     )
-    sub = iota((8, 256), 0)
+    sub = iota((16, 256), 0)
 
     def group(g, _):
-        named = [sid_ref[k : k + 1, :] - g * 256 for k in range(8)]
+        named = jnp.clip(sid_ref[:8, :] - g * 256, -1, 256).astype(f32).astype(bf16)
+        named = [jnp.broadcast_to(named[k : k + 1], (16, 256)) for k in range(8)]
         strips = []
         for i in range(12):
-            tiles = []
-            for q in (2 * i, 2 * i + 1):
-                first = (q // 3) * SLOTS + (q % 3) * 8
-                mask = sub == named[0] - first
-                for k in range(1, 8):
-                    mask = mask | (sub == named[k] - first)
-                tiles.append(jnp.where(mask, 1.0, 0.0))
-            strips.append(jnp.concatenate(tiles, axis=0).astype(bf16))
+            places = [(q // 3) * SLOTS + (q % 3) * 8 for q in (2 * i, 2 * i + 1)]
+            at = (jnp.where(sub < 8, places[0], places[1] - 8) + sub).astype(f32).astype(bf16)
+            mask = at == named[0]
+            for k in range(1, 8):
+                mask = mask | (at == named[k])
+            strips.append(one16(mask))
         rows = dot(jnp.concatenate(strips, axis=0), q_ref[...])
         left = rows[:, :128].reshape(GROUP, PAIRS, 128)
         right = rows[:, 128:].reshape(GROUP, PAIRS, 128)
@@ -175,7 +178,7 @@
 
     lax.fori_loop(0, NGROUPS, take, 0, unroll=16)
     ext = ext_scr[pl.ds(0, 128, stride=8), :]
-    flag_ref[0, 0] = jnp.max(ext[:, 64:65])
+    flag_ref[0, 0] = jnp.max(ext[:, 64:65]).astype(i32)
     source, col = iota((128, 256), 0), iota((128, 256), 1)
     owner_of = jnp.floor((col.astype(f32) + 0.5) / PAIRS).astype(i32)
     spread = one(source == col - owner_of * PAIRS)
@@ -608,7 +611,7 @@
     x, slot_target, flag, stat, send = pl.pallas_call(
         owner_kernel,
         out_shape=(
-            pltpu.HBM((16, 256, 256), bf16), pltpu.VMEM((256, 128), f32), shape(1, 1), pltpu.VMEM((256, 128), f32),
+            pltpu.HBM((16, 256, 256), bf16), pltpu.VMEM((256, 128), f32), shape(1, 1, dtype=i32), pltpu.VMEM((256, 128), f32),
             pltpu.HBM((DEVS * BACK, 128), bf16),
         ),
         in_specs=[SMEM, VMEM, VMEM, HBM],
@@ -635,7 +638,7 @@
     def packed():
         return finish(queries, counts, labels, accum, sid, x, slot_target, stat, send)
 
-    return lax.cond(flag[0, 0] > 0.5, plain, packed)
+    return lax.switch(flag[0, 0], [packed, plain])
 
 
 def finish(queries, counts, labels, accum, sid, x, slot_target, stat, send):

time: 113 us -> 112 us (level)
  Pallas kernels: 40.5 us -> 39 us
    pallas_call x1, Pallas kernels: 6.01 us -> 4.6 us  [shards(): pl.pallas_call(route_kernel, out_shape=(pltpu.HBM((DEVS * OUT, 128), bf16...]
where the time goes in v4:
time: 112 us; the launch traced here: 111 us
  waiting for transfers between devices  46.9 us (42%)
  Pallas kernels  39 us (35%)
  starting transfers between devices  20.5 us (18%)
  local copies, waits for them, and re-layouts  2.95 us (3%)
  between operations  1.61 us (1%)
    all_to_all x3, waiting for transfers between devices, exchange(): return lax.all_to_all(x, 'shard', split_axis=0, concat_axis=0, tiled=True)  46.9 us
    all_to_all x3, starting transfers between devices, exchange(): return lax.all_to_all(x, 'shard', split_axis=0, concat_axis=0, tiled=True)  20.5 us
    pallas_call x1, Pallas kernels, finish(): pl.pallas_call(ready_kernel, out_shape=(pltpu.VMEM((NGROUPS, 256, 256), b...  13.9 us
    pallas_call x1, Pallas kernels, shards(): pl.pallas_call(owner_kernel, out_shape=(pltpu.HBM((16, 256, 256), bf16),...  8.99 us
    pallas_call x1, Pallas kernels, finish(): pl.pallas_call(table_kernel, out_shape=(pltpu.HBM((16, 256, 256), f32), p...  5.68 us
    pallas_call x1, Pallas kernels, shards(): pl.pallas_call(route_kernel, out_shape=(pltpu.HBM((DEVS * OUT, 128), bf16...  4.6 us
    pallas_call x1, Pallas kernels, finish(): pl.pallas_call(combine_kernel, out_shape=(pltpu.HBM((256, 256), bf16), pl...  3.75 us
    cond x4, local copies, waits for them, and re-layouts  2.9 us
  transfers between devices with their start and end apart: 3, of which 3 were waited for; matrix products, arithmetic and copies ran while one was open for 0% of the time, Pallas kernels for 16%

profile of v4, /device:TPU:1, one launch (start us, length us, event | category | flops | bytes accessed | tf_op | source)
XLA Modules:
  0.0 111.4 jit_solution(11143650483137246433)
XLA Ops:
  0.6 0.0 copy-start.24
  0.6 4.6 %route.1 = (bf16[7168,128]{1,0:T(8,128)(2,1)}, s32[24,256]{1,0:T(8,128)S(1)}) custom-call(s32[8,256]{1,0:T(8,128)} %bitcast.53, s32[16,128]{1,0:T(8,128)} %bitcast.47, s32[1,256]{1,0:T(1,128)} %bitcast.55, s32[1,256]{1,0:T(1,128)} %bitcast.56, bf16[256,256]{1,0:T(8,128)(2,1)} %q_any.1), custom_call_target="tpu_custom_call" | custom-call | tf_op jit(solution)/shard_map/route/pallas_call | solution.py:587
  5.2 11.5 %all-to-all-start.10 = ((bf16[128,56,128]{2,1,0:T(8,128)(2,1)}), bf16[128,56,128]{2,1,0:T(8,128)(2,1)S(1)}, u32[]{:S(2)}, u32[]{:S(2)}) async-start(bf16[128,56,128]{2,1,0:T(8,128)(2,1)} %bitcast.49), calls=%async_computation.10 | async-start | bytes 3670016 | tf_op jit(solution)/shard_map/all_to_all | solution.py:460
  16.8 0.0 copy-done.24
  16.8 0.0 copy-start.2
  16.8 0.0 copy-start.6
  16.8 0.0 copy-start.17
  16.8 0.0 copy-start.20
  16.8 0.0 copy-start.25
  16.8 0.0 copy-start.26
  16.9 27.4 %all-to-all-done.10 = bf16[128,56,128]{2,1,0:T(8,128)(2,1)S(1)} async-done(((bf16[128,56,128]{2,1,0:T(8,128)(2,1)}), bf16[128,56,128]{2,1,0:T(8,128)(2,1)S(1)}, u32[]{:S(2)}, u32[]{:S(2)}) %all-to-all-start.10) | async-done | bytes 1835040 | tf_op jit(solution)/shard_map/all_to_all | solution.py:460
  44.3 9.0 %owner.1 = (bf16[16,256,256]{2,1,0:T(8,128)(2,1)}, f32[256,128]{1,0:T(8,128)S(1)}, s32[1,1]{1,0:T(1,128)}, f32[256,128]{1,0:T(8,128)S(1)}, bf16[8192,128]{1,0:T(8,128)(2,1)}) custom-call(s32[16]{0:T(128)S(1)} %copy-done.24, f32[1,128]{1,0:T(1,128)S(1)} %pad_bitcast_fusion.cc_ref, bf16[7168,128]{1,0:T(8,128)(2,1)S(1)} %bitcast.45, bf16[16,256,256]{2,1,0:T(8,128)(2,1)} %lab_any.1), custom_call_target="tpu_custom_call" | custom-call | tf_op jit(solution)/shard_map/owner/pallas_call | solution.py:611
  53.9 0.0 copy-done.2
  53.9 0.0 copy-done.6
  53.9 0.0 copy-done.17
  54.0 0.0 copy-done.20
  54.0 0.0 copy-done.25
  54.0 0.0 copy-done.26
  54.0 57.2 %conditional.1 = (f32[16,256]{1,0:T(8,128)}, bf16[256,256]{1,0:T(8,128)(2,1)}, f32[256]{0:T(256)}, f32[16,256,256]{2,1,0:T(8,128)}) conditional(s32[]{:T(128)} %bitcast.24, (bf16[8192,128]{1,0:T(8,128)(2,1)}, s32[24,256]{1,0:T(8,128)S(1)}, s32[16]{0:T(128)S(1)}, f32[256,128]{1,0:T(8,128)S(1)}, f32[256,128]{1,0:T(8,128)S(1)}, ...), branch_computations={%region_0.0_spmd, %region_1.18_spmd} | conditional | flops 2177789952 | bytes 174500992 | solution.py:641
  54.0 4.6 %all-to-all-start = ((bf16[128,64,128]{2,1,0:T(8,128)(2,1)}), bf16[128,64,128]{2,1,0:T(8,128)(2,1)S(1)}, u32[]{:S(2)}, u32[]{:S(2)}) async-start(bf16[128,64,128]{2,1,0:T(8,128)(2,1)} %bitcast.48), calls=%async_computation | async-start | bytes 4194304 | tf_op jit(solution)/shard_map/cond/branch_0_fun/all_to_all | solution.py:460
  58.6 13.9 %ready.1 = (bf16[16,256,256]{2,1,0:T(8,128)(2,1)S(1)}, f32[256,128]{1,0:T(8,128)S(1)}, f32[16,256]{1,0:T(8,128)S(1)}, f32[16,256]{1,0:T(8,128)S(1)}, f32[16,256,256]{2,1,0:T(8,128)}) custom-call(s32[16]{0:T(128)S(1)} %get-tuple-element.37.counts_ref, s32[24,256]{1,0:T(8,128)S(1)} %get-tuple-element.35.sid_ref, f32[256,128]{1,0:T(8,128)S(1)} %get-tuple-element.38.stat_ref, ...), custom_call_target="tpu_custom_call" | custom-call | flops 536870912 | bytes 10000000 | tf_op jit(solution)/shard_map/cond/branch_0_fun/ready/pallas_call | solution.py:646
  72.6 0.0 copy-start
  72.6 1.3 %copy-done = bf16[16,256,256]{2,1,0:T(8,128)(2,1)} copy-done((bf16[16,256,256]{2,1,0:T(8,128)(2,1)}, bf16[16,256,256]{2,1,0:T(8,128)(2,1)S(1)}, u32[]{:S(2)}) %copy-start) | copy-done | bytes 2097176 | tf_op jit(solution)/shard_map/cond
  73.9 15.3 %all-to-all-done = bf16[128,64,128]{2,1,0:T(8,128)(2,1)S(1)} async-done(((bf16[128,64,128]{2,1,0:T(8,128)(2,1)}), bf16[128,64,128]{2,1,0:T(8,128)(2,1)S(1)}, u32[]{:S(2)}, u32[]{:S(2)}) %all-to-all-start) | async-done | bytes 2097184 | tf_op jit(solution)/shard_map/cond/branch_0_fun/all_to_all | solution.py:460
  89.1 2.1 %normalizer.1 = (f32[1,256]{1,0:T(1,128)S(1)}, f32[128,128]{1,0:T(8,128)}, f32[128,128]{1,0:T(8,128)S(1)}) custom-call(bf16[8192,128]{1,0:T(8,128)(2,1)S(1)} %bitcast.43, s32[24,256]{1,0:T(8,128)S(1)} %get-tuple-element.35.sid_ref), custom_call_target="tpu_custom_call" | custom-call | tf_op jit(solution)/shard_map/cond/branch_0_fun/normalizer/pallas_call | solution.py:664
  91.2 4.4 %all-to-all-start.1 = ((f32[128,1,128]{2,1,0:T(1,128)}), f32[128,1,128]{2,1,0:T(1,128)S(1)}, u32[]{:S(2)}, u32[]{:S(2)}) async-start(f32[128,1,128]{2,1,0:T(1,128)} %bitcast.3), calls=%async_computation.1 | async-start | bytes 131072 | tf_op jit(solution)/shard_map/cond/branch_0_fun/all_to_all | solution.py:460
  95.6 0.0 copy-start.1
  95.7 1.6 %copy-done.1 = bf16[16,256,256]{2,1,0:T(8,128)(2,1)S(1)} copy-done((bf16[16,256,256]{2,1,0:T(8,128)(2,1)S(1)}, bf16[16,256,256]{2,1,0:T(8,128)(2,1)}, u32[]{:S(2)}) %copy-start.1) | copy-done | bytes 2097176 | tf_op jit(solution)/shard_map/cond
  97.2 3.8 %combine.1 = (bf16[256,256]{1,0:T(8,128)(2,1)}, f32[1,256]{1,0:T(1,128)}) custom-call(bf16[8192,128]{1,0:T(8,128)(2,1)S(1)} %bitcast.44, bf16[16,256,256]{2,1,0:T(8,128)(2,1)S(1)} %copy-done.1, f32[128,128]{1,0:T(8,128)S(1)} %get-tuple-element.50.scale_ref, f32[1,256]{1,0:T(1,128)S(1)} %get-tuple-element.51.lse_ref, bf16[256,256]{1,0:T(8,128)(2,1)S(1)} %get-tuple-element.52.q_ref), custom_call_target="tpu_custom_call" | custom-call | flops 1073741824 | bytes 5000000 | tf_op jit(solution)/shard_map/cond/branch_0_fun/combine/pallas_call | solution.py:674
  101.0 4.3 %all-to-all-done.1 = f32[128,1,128]{2,1,0:T(1,128)S(1)} async-done(((f32[128,1,128]{2,1,0:T(1,128)}), f32[128,1,128]{2,1,0:T(1,128)S(1)}, u32[]{:S(2)}, u32[]{:S(2)}) %all-to-all-start.1) | async-done | bytes 65568 | tf_op jit(solution)/shard_map/cond/branch_0_fun/all_to_all | solution.py:460
  105.3 5.7 %table.1 = (f32[16,256,256]{2,1,0:T(8,128)}, f32[16,256]{1,0:T(8,128)}) custom-call(f32[128,128]{1,0:T(8,128)S(1)} %bitcast.46, f32[16,256]{1,0:T(8,128)S(1)} %get-tuple-element.43.top_ref, f32[16,256]{1,0:T(8,128)S(1)} %get-tuple-element.44.tr_ref, f32[256,128]{1,0:T(8,128)S(1)} %get-tuple-element.45.acct_ref, ...), custom_call_target="tpu_custom_call" | custom-call | tf_op jit(solution)/shard_map/cond/branch_0_fun/table/pallas_call | solution.py:686
  (2 shorter events, 0.0 us)
Async XLA Ops:
  0.6 16.1 %copy-start.24 = (s32[16]{0:T(128)S(1)}, s32[16]{0:T(128)}, u32[]{:S(2)}) copy-start(s32[16]{0:T(128)} %counts_ref.1) | copy-start | bytes 196
  5.2 39.0 %all-to-all-start.10 = ((bf16[128,56,128]{2,1,0:T(8,128)(2,1)}), bf16[128,56,128]{2,1,0:T(8,128)(2,1)S(1)}, u32[]{:S(2)}, u32[]{:S(2)}) async-start(bf16[128,56,128]{2,1,0:T(8,128)(2,1)} %bitcast.49), calls=%async_computation.10 | async-start | bytes 3670016 | tf_op jit(solution)/shard_map/all_to_all | solution.py:460
  16.8 37.2 %copy-start.2 = (s32[2048]{0:T(1024)S(1)}, s32[2048]{0:T(1024)}, u32[]{:S(2)}) copy-start(s32[2048]{0:T(1024)} %param.12) | copy-start | bytes 24580
  16.8 37.2 %copy-start.6 = (bf16[256,256]{1,0:T(8,128)(2,1)S(1)}, bf16[256,256]{1,0:T(8,128)(2,1)}, u32[]{:S(2)}) copy-start(bf16[256,256]{1,0:T(8,128)(2,1)} %q_any.1) | copy-start | bytes 393220
  16.8 37.2 %copy-start.17 = (f32[16,256]{1,0:T(8,128)S(1)}, f32[16,256]{1,0:T(8,128)}, u32[]{:S(2)}) copy-start(f32[16,256]{1,0:T(8,128)} %param.17) | copy-start | bytes 49156
  16.8 37.2 %copy-start.20 = (s32[256,8]{0,1:T(8,128)S(1)}, s32[256,8]{0,1:T(8,128)}, u32[]{:S(2)}) copy-start(s32[256,8]{0,1:T(8,128)} %param.11) | copy-start | bytes 24580
  16.8 37.1 %copy-start.25 = (s32[256]{0:T(256)S(1)}, s32[256]{0:T(256)}, u32[]{:S(2)}) copy-start(s32[256]{0:T(256)} %param.13) | copy-start | bytes 3076
  16.8 37.1 %copy-start.26 = (s32[256]{0:T(256)S(1)}, s32[256]{0:T(256)}, u32[]{:S(2)}) copy-start(s32[256]{0:T(256)} %param.14) | copy-start | bytes 3076
  54.0 35.1 %all-to-all-start = ((bf16[128,64,128]{2,1,0:T(8,128)(2,1)}), bf16[128,64,128]{2,1,0:T(8,128)(2,1)S(1)}, u32[]{:S(2)}, u32[]{:S(2)}) async-start(bf16[128,64,128]{2,1,0:T(8,128)(2,1)} %bitcast.48), calls=%async_computation | async-start | bytes 4194304 | tf_op jit(solution)/shard_map/cond/branch_0_fun/all_to_all | solution.py:460
  72.6 1.3 %copy-start = (bf16[16,256,256]{2,1,0:T(8,128)(2,1)}, bf16[16,256,256]{2,1,0:T(8,128)(2,1)S(1)}, u32[]{:S(2)}) copy-start(bf16[16,256,256]{2,1,0:T(8,128)(2,1)S(1)} %get-tuple-element.49.mask_ref) | copy-start | bytes 6291460 | tf_op jit(solution)/shard_map/cond
  91.2 14.1 %all-to-all-start.1 = ((f32[128,1,128]{2,1,0:T(1,128)}), f32[128,1,128]{2,1,0:T(1,128)S(1)}, u32[]{:S(2)}, u32[]{:S(2)}) async-start(f32[128,1,128]{2,1,0:T(1,128)} %bitcast.3), calls=%async_computation.1 | async-start | bytes 131072 | tf_op jit(solution)/shard_map/cond/branch_0_fun/all_to_all | solution.py:460
  95.6 1.6 %copy-start.1 = (bf16[16,256,256]{2,1,0:T(8,128)(2,1)S(1)}, bf16[16,256,256]{2,1,0:T(8,128)(2,1)}, u32[]{:S(2)}) copy-start(bf16[16,256,256]{2,1,0:T(8,128)(2,1)} %copy-done) | copy-start | bytes 6291460 | tf_op jit(solution)/shard_map/cond

commit v5 on v4

--- a/solution.py
+++ b/solution.py
@@ -267,7 +267,7 @@
         send_block(send_ref, send_any, out_sems, g, BACK).start()
         return 0
 
-    lax.fori_loop(0, NGROUPS, scatter, 0, unroll=8)
+    lax.fori_loop(0, NGROUPS, scatter, 0, unroll=16)
     x_copy.wait()
     for g in range(NGROUPS):
         send_block(send_ref, send_any, out_sems, g, BACK).wait()
@@ -306,6 +306,15 @@
     copy.wait()
 
 
+def spread_pairs(values, rows, ohs):
+    i32s = iota((32, 256), 0)
+    outs = []
+    for value, row, _ in zip(values, rows, ohs):
+        outs.append(jnp.concatenate([jnp.where(i32s == row, p, 0.0) for p in pieces_of(value)], axis=0).astype(bf16))
+    out = dot(jnp.concatenate(outs, axis=1), jnp.concatenate(ohs, axis=1), 1, 1)
+    return out[:32] + out[32:64] + out[64:]
+
+
 def lse_kernel(recv_ref, sid_ref, lse_ref, send_ref, scale_ref, left_scr, right_scr):
     def take(g, _):
         block = from_rows(recv_ref, g, BACK)
@@ -317,7 +326,7 @@
     lax.fori_loop(0, NGROUPS, take, 0, unroll=16)
     stats = [scr[pl.ds(7, 128, stride=8), :].T for scr in (left_scr, right_scr)]
     table = jnp.concatenate(stats, axis=0).astype(bf16)
-    i128, i16, i32s = iota((128, 256), 0), iota((16, 256), 0), iota((32, 256), 0)
+    i128, i16 = iota((128, 256), 0), iota((16, 256), 0)
     sid = sid_ref[...]
     tops, sums, ohs = [], [], []
     for k in range(8):
@@ -337,25 +346,20 @@
         norm = norm + sums[k] * jnp.exp(tops[k] - largest)
     lse = largest + jnp.log(norm)
     lse_ref[...] = lse
-    split = pieces_of(lse)
-    outs = []
-    for k in range(8):
-        j, rl = sid[k : k + 1] & 31, sid[8 + k : 9 + k]
-        w = [jnp.where(i32s == rl, p, 0.0) for p in split]
-        w += [jnp.where(i32s == j, p, 0.0) for p in pieces_of(jnp.exp(tops[k] - lse))]
-        outs.append(jnp.concatenate(w, axis=0).astype(bf16))
-    out = dot(jnp.concatenate(outs, axis=1), jnp.concatenate(ohs, axis=1), 1, 1)
-    out = jnp.concatenate([out[:32] + out[32:64] + out[64:96], out[96:128] + out[128:160] + out[160:]], axis=0)
-    out = jnp.concatenate([out, jnp.zeros((64, 128), f32)], axis=0).T
-    send_ref[...] = out
-    scale_ref[...] = jnp.where(iota((128, 128), 1) < 32, pltpu.roll(out, 96, 1), 0.0)
-
-
-def combine_kernel(recv_ref, mask_ref, scale_ref, lse_ref, q_ref, out_ref, loss_ref, row_scr):
+    scale_ref[...] = jnp.concatenate([jnp.exp(t - lse) for t in tops], axis=0)
+    out = spread_pairs([lse] * 8, [sid[8 + k : 9 + k] for k in range(8)], ohs)
+    send_ref[...] = jnp.concatenate([out, jnp.zeros((96, 128), f32)], axis=0).T
+
+
+def combine_kernel(recv_ref, mask_ref, scale_ref, sid_ref, lse_ref, q_ref, out_ref, loss_ref, row_scr):
+    sid = sid_ref[...]
+    ohs = [one(iota((128, 256), 0) == (sid[k : k + 1] >> 5)) for k in range(8)]
+    scales = spread_pairs([scale_ref[k : k + 1, :] for k in range(8)], [sid[k : k + 1] & 31 for k in range(8)], ohs)
+    scales = jnp.concatenate([scales, jnp.zeros((96, 128), f32)], axis=0).T
     r256, c256 = iota((128, 256), 0), iota((128, 256), 1)
     spread = one((r256 == (c256 & 31)) & (r256 < 32))
     wide = jnp.zeros((128, 256), f32)
-    for piece in pieces_of(scale_ref[...]):
+    for piece in pieces_of(scales):
         wide = wide + dot(piece.astype(bf16), spread)
     wide = jnp.where((r256 & 7) == (c256 >> 5), wide, 0.0)
     row_scr[...] = jnp.sum(wide.reshape(NGROUPS, GROUP, 256), axis=1)
@@ -663,7 +667,7 @@
     )(counts, sid, stat, slot_target, accum, in_hbm(x), in_hbm(labels))
     lse, send, scale = pl.pallas_call(
         lse_kernel,
-        out_shape=(shape(1, 256), shape(DEVS, 128), shape(DEVS, 128)),
+        out_shape=(shape(1, 256), shape(DEVS, 128), shape(8, 256)),
         in_specs=[VMEM, VMEM],
         out_specs=(VMEM,) * 3,
         scratch_shapes=[pltpu.VMEM((1024, 128), f32)] * 2,
@@ -674,7 +678,7 @@
     query_grad, loss = pl.pallas_call(
         combine_kernel,
         out_shape=(pltpu.HBM((256, 256), bf16), pltpu.HBM((1, 256), f32)),
-        in_specs=[VMEM] * 5,
+        in_specs=[VMEM] * 6,
         out_specs=(VMEM, VMEM),
         scratch_shapes=[
             pltpu.VMEM((NGROUPS, 256), f32),
@@ -682,7 +686,7 @@
         compiler_params=params(8),
         cost_estimate=pl.CostEstimate(flops=2 * 2 * 256 * 4096 * 256, bytes_accessed=5_000_000, transcendentals=256 * 4096),
         name="combine",
-    )(recv, mask, scale, lse, queries)
+    )(recv, mask, scale, sid, lse, queries)
     new_labels, new_accum = pl.pallas_call(
         table_kernel,
         out_shape=(pltpu.HBM((16, 256, 256), f32), pltpu.HBM((16, 256), f32)),

time: 112 us -> 111 us (level)
  no operation moved by 1% of the time
where the time goes in v5:
time: 111 us
  waiting for transfers between devices  46.5 us (42%)
  Pallas kernels  39.1 us (35%)
  starting transfers between devices  20.5 us (18%)
  local copies, waits for them, and re-layouts  2.95 us (3%)
  between operations  1.61 us (1%)
    all_to_all x3, waiting for transfers between devices, exchange(): return lax.all_to_all(x, 'shard', split_axis=0, concat_axis=0, tiled=True)  46.5 us
    all_to_all x3, starting transfers between devices, exchange(): return lax.all_to_all(x, 'shard', split_axis=0, concat_axis=0, tiled=True)  20.5 us
    pallas_call x1, Pallas kernels, finish(): pl.pallas_call(ready_kernel, out_shape=(pltpu.VMEM((NGROUPS, 256, 256), b...  13.9 us
    pallas_call x1, Pallas kernels, shards(): pl.pallas_call(owner_kernel, out_shape=(pltpu.HBM((16, 256, 256), bf16),...  8.84 us
    pallas_call x1, Pallas kernels, finish(): pl.pallas_call(table_kernel, out_shape=(pltpu.HBM((16, 256, 256), f32), p...  5.7 us
    pallas_call x1, Pallas kernels, shards(): pl.pallas_call(route_kernel, out_shape=(pltpu.HBM((DEVS * OUT, 128), bf16...  4.6 us
    pallas_call x1, Pallas kernels, finish(): pl.pallas_call(combine_kernel, out_shape=(pltpu.HBM((256, 256), bf16), pl...  4.2 us
    cond x4, local copies, waits for them, and re-layouts  2.9 us
  transfers between devices with their start and end apart: 3, of which 3 were waited for; matrix products, arithmetic and copies ran while one was open for 0% of the time, Pallas kernels for 16%

profile of v5, /device:TPU:1, one launch (start us, length us, event | category | flops | bytes accessed | tf_op | source)
XLA Modules:
  0.0 111.0 jit_solution(17901412610942848484)
XLA Ops:
  0.6 0.0 copy-start.24
  0.6 4.6 %route.1 = (bf16[7168,128]{1,0:T(8,128)(2,1)}, s32[24,256]{1,0:T(8,128)S(1)}) custom-call(s32[8,256]{1,0:T(8,128)} %bitcast.53, s32[16,128]{1,0:T(8,128)} %bitcast.47, s32[1,256]{1,0:T(1,128)} %bitcast.55, s32[1,256]{1,0:T(1,128)} %bitcast.56, bf16[256,256]{1,0:T(8,128)(2,1)} %q_any.1), custom_call_target="tpu_custom_call" | custom-call | tf_op jit(solution)/shard_map/route/pallas_call | solution.py:591
  5.2 11.5 %all-to-all-start.10 = ((bf16[128,56,128]{2,1,0:T(8,128)(2,1)}), bf16[128,56,128]{2,1,0:T(8,128)(2,1)S(1)}, u32[]{:S(2)}, u32[]{:S(2)}) async-start(bf16[128,56,128]{2,1,0:T(8,128)(2,1)} %bitcast.49), calls=%async_computation.10 | async-start | bytes 3670016 | tf_op jit(solution)/shard_map/all_to_all | solution.py:464
  16.8 0.0 copy-done.24
  16.8 0.0 copy-start.2
  16.8 0.0 copy-start.6
  16.8 0.0 copy-start.17
  16.8 0.0 copy-start.20
  16.8 0.0 copy-start.25
  16.8 0.0 copy-start.26
  16.9 27.4 %all-to-all-done.10 = bf16[128,56,128]{2,1,0:T(8,128)(2,1)S(1)} async-done(((bf16[128,56,128]{2,1,0:T(8,128)(2,1)}), bf16[128,56,128]{2,1,0:T(8,128)(2,1)S(1)}, u32[]{:S(2)}, u32[]{:S(2)}) %all-to-all-start.10) | async-done | bytes 1835040 | tf_op jit(solution)/shard_map/all_to_all | solution.py:464
  44.3 8.8 %owner.1 = (bf16[16,256,256]{2,1,0:T(8,128)(2,1)}, f32[256,128]{1,0:T(8,128)S(1)}, s32[1,1]{1,0:T(1,128)}, f32[256,128]{1,0:T(8,128)S(1)}, bf16[8192,128]{1,0:T(8,128)(2,1)}) custom-call(s32[16]{0:T(128)S(1)} %copy-done.24, f32[1,128]{1,0:T(1,128)S(1)} %pad_bitcast_fusion.cc_ref, bf16[7168,128]{1,0:T(8,128)(2,1)S(1)} %bitcast.45, bf16[16,256,256]{2,1,0:T(8,128)(2,1)} %lab_any.1), custom_call_target="tpu_custom_call" | custom-call | tf_op jit(solution)/shard_map/owner/pallas_call | solution.py:615
  53.8 0.0 copy-done.2
  53.8 0.0 copy-done.6
  53.8 0.0 copy-done.17
  53.8 0.0 copy-done.20
  53.8 0.0 copy-done.25
  53.8 0.0 copy-done.26
  53.8 57.0 %conditional.1 = (f32[16,256]{1,0:T(8,128)}, bf16[256,256]{1,0:T(8,128)(2,1)}, f32[256]{0:T(256)}, f32[16,256,256]{2,1,0:T(8,128)}) conditional(s32[]{:T(128)} %bitcast.24, (bf16[8192,128]{1,0:T(8,128)(2,1)}, s32[24,256]{1,0:T(8,128)S(1)}, s32[16]{0:T(128)S(1)}, f32[256,128]{1,0:T(8,128)S(1)}, f32[256,128]{1,0:T(8,128)S(1)}, ...), branch_computations={%region_0.0_spmd, %region_1.18_spmd} | conditional | flops 2177789952 | bytes 174500992 | solution.py:645
  53.8 4.6 %all-to-all-start = ((bf16[128,64,128]{2,1,0:T(8,128)(2,1)}), bf16[128,64,128]{2,1,0:T(8,128)(2,1)S(1)}, u32[]{:S(2)}, u32[]{:S(2)}) async-start(bf16[128,64,128]{2,1,0:T(8,128)(2,1)} %bitcast.48), calls=%async_computation | async-start | bytes 4194304 | tf_op jit(solution)/shard_map/cond/branch_0_fun/all_to_all | solution.py:464
  58.5 13.9 %ready.1 = (bf16[16,256,256]{2,1,0:T(8,128)(2,1)S(1)}, f32[256,128]{1,0:T(8,128)S(1)}, f32[16,256]{1,0:T(8,128)S(1)}, f32[16,256]{1,0:T(8,128)S(1)}, f32[16,256,256]{2,1,0:T(8,128)}) custom-call(s32[16]{0:T(128)S(1)} %get-tuple-element.37.counts_ref, s32[24,256]{1,0:T(8,128)S(1)} %get-tuple-element.35.sid_ref, f32[256,128]{1,0:T(8,128)S(1)} %get-tuple-element.38.stat_ref, ...), custom_call_target="tpu_custom_call" | custom-call | flops 536870912 | bytes 10000000 | tf_op jit(solution)/shard_map/cond/branch_0_fun/ready/pallas_call | solution.py:650
  72.4 0.0 copy-start
  72.4 1.3 %copy-done = bf16[16,256,256]{2,1,0:T(8,128)(2,1)} copy-done((bf16[16,256,256]{2,1,0:T(8,128)(2,1)}, bf16[16,256,256]{2,1,0:T(8,128)(2,1)S(1)}, u32[]{:S(2)}) %copy-start) | copy-done | bytes 2097176 | tf_op jit(solution)/shard_map/cond
  73.7 15.3 %all-to-all-done = bf16[128,64,128]{2,1,0:T(8,128)(2,1)S(1)} async-done(((bf16[128,64,128]{2,1,0:T(8,128)(2,1)}), bf16[128,64,128]{2,1,0:T(8,128)(2,1)S(1)}, u32[]{:S(2)}, u32[]{:S(2)}) %all-to-all-start) | async-done | bytes 2097184 | tf_op jit(solution)/shard_map/cond/branch_0_fun/all_to_all | solution.py:464
  89.0 1.8 %normalizer.1 = (f32[1,256]{1,0:T(1,128)S(1)}, f32[128,128]{1,0:T(8,128)}, f32[8,256]{1,0:T(8,128)S(1)}) custom-call(bf16[8192,128]{1,0:T(8,128)(2,1)S(1)} %bitcast.43, s32[24,256]{1,0:T(8,128)S(1)} %get-tuple-element.35.sid_ref), custom_call_target="tpu_custom_call" | custom-call | tf_op jit(solution)/shard_map/cond/branch_0_fun/normalizer/pallas_call | solution.py:668
  90.8 4.4 %all-to-all-start.1 = ((f32[128,1,128]{2,1,0:T(1,128)}), f32[128,1,128]{2,1,0:T(1,128)S(1)}, u32[]{:S(2)}, u32[]{:S(2)}) async-start(f32[128,1,128]{2,1,0:T(1,128)} %bitcast.3), calls=%async_computation.1 | async-start | bytes 131072 | tf_op jit(solution)/shard_map/cond/branch_0_fun/all_to_all | solution.py:464
  95.3 0.0 copy-start.1
  95.3 1.6 %copy-done.1 = bf16[16,256,256]{2,1,0:T(8,128)(2,1)S(1)} copy-done((bf16[16,256,256]{2,1,0:T(8,128)(2,1)S(1)}, bf16[16,256,256]{2,1,0:T(8,128)(2,1)}, u32[]{:S(2)}) %copy-start.1) | copy-done | bytes 2097176 | tf_op jit(solution)/shard_map/cond
  96.9 4.2 %combine.1 = (bf16[256,256]{1,0:T(8,128)(2,1)}, f32[1,256]{1,0:T(1,128)}) custom-call(bf16[8192,128]{1,0:T(8,128)(2,1)S(1)} %bitcast.44, bf16[16,256,256]{2,1,0:T(8,128)(2,1)S(1)} %copy-done.1, f32[8,256]{1,0:T(8,128)S(1)} %get-tuple-element.50.scale_ref, s32[24,256]{1,0:T(8,128)S(1)} %get-tuple-element.35.sid_ref, f32[1,256]{1,0:T(1,128)S(1)} %get-tuple-element.51.lse_ref, ...), custom_call_target="tpu_custom_call" | custom-call | flops 1073741824 | bytes 5000000 | tf_op jit(solution)/shard_map/cond/branch_0_fun/combine/pallas_call | solution.py:678
  101.1 3.8 %all-to-all-done.1 = f32[128,1,128]{2,1,0:T(1,128)S(1)} async-done(((f32[128,1,128]{2,1,0:T(1,128)}), f32[128,1,128]{2,1,0:T(1,128)S(1)}, u32[]{:S(2)}, u32[]{:S(2)}) %all-to-all-start.1) | async-done | bytes 65568 | tf_op jit(solution)/shard_map/cond/branch_0_fun/all_to_all | solution.py:464
  104.9 5.7 %table.1 = (f32[16,256,256]{2,1,0:T(8,128)}, f32[16,256]{1,0:T(8,128)}) custom-call(f32[128,128]{1,0:T(8,128)S(1)} %bitcast.46, f32[16,256]{1,0:T(8,128)S(1)} %get-tuple-element.43.top_ref, f32[16,256]{1,0:T(8,128)S(1)} %get-tuple-element.44.tr_ref, f32[256,128]{1,0:T(8,128)S(1)} %get-tuple-element.45.acct_ref, ...), custom_call_target="tpu_custom_call" | custom-call | tf_op jit(solution)/shard_map/cond/branch_0_fun/table/pallas_call | solution.py:690
  (2 shorter events, 0.0 us)
Async XLA Ops:
  0.6 16.1 %copy-start.24 = (s32[16]{0:T(128)S(1)}, s32[16]{0:T(128)}, u32[]{:S(2)}) copy-start(s32[16]{0:T(128)} %counts_ref.1) | copy-start | bytes 196
  5.2 39.0 %all-to-all-start.10 = ((bf16[128,56,128]{2,1,0:T(8,128)(2,1)}), bf16[128,56,128]{2,1,0:T(8,128)(2,1)S(1)}, u32[]{:S(2)}, u32[]{:S(2)}) async-start(bf16[128,56,128]{2,1,0:T(8,128)(2,1)} %bitcast.49), calls=%async_computation.10 | async-start | bytes 3670016 | tf_op jit(solution)/shard_map/all_to_all | solution.py:464
  16.8 37.0 %copy-start.2 = (s32[2048]{0:T(1024)S(1)}, s32[2048]{0:T(1024)}, u32[]{:S(2)}) copy-start(s32[2048]{0:T(1024)} %param.12) | copy-start | bytes 24580
  16.8 37.0 %copy-start.6 = (bf16[256,256]{1,0:T(8,128)(2,1)S(1)}, bf16[256,256]{1,0:T(8,128)(2,1)}, u32[]{:S(2)}) copy-start(bf16[256,256]{1,0:T(8,128)(2,1)} %q_any.1) | copy-start | bytes 393220
  16.8 37.0 %copy-start.17 = (f32[16,256]{1,0:T(8,128)S(1)}, f32[16,256]{1,0:T(8,128)}, u32[]{:S(2)}) copy-start(f32[16,256]{1,0:T(8,128)} %param.17) | copy-start | bytes 49156
  16.8 37.0 %copy-start.20 = (s32[256,8]{0,1:T(8,128)S(1)}, s32[256,8]{0,1:T(8,128)}, u32[]{:S(2)}) copy-start(s32[256,8]{0,1:T(8,128)} %param.11) | copy-start | bytes 24580
  16.8 37.0 %copy-start.25 = (s32[256]{0:T(256)S(1)}, s32[256]{0:T(256)}, u32[]{:S(2)}) copy-start(s32[256]{0:T(256)} %param.13) | copy-start | bytes 3076
  16.8 37.0 %copy-start.26 = (s32[256]{0:T(256)S(1)}, s32[256]{0:T(256)}, u32[]{:S(2)}) copy-start(s32[256]{0:T(256)} %param.14) | copy-start | bytes 3076
  53.8 35.1 %all-to-all-start = ((bf16[128,64,128]{2,1,0:T(8,128)(2,1)}), bf16[128,64,128]{2,1,0:T(8,128)(2,1)S(1)}, u32[]{:S(2)}, u32[]{:S(2)}) async-start(bf16[128,64,128]{2,1,0:T(8,128)(2,1)} %bitcast.48), calls=%async_computation | async-start | bytes 4194304 | tf_op jit(solution)/shard_map/cond/branch_0_fun/all_to_all | solution.py:464
  72.4 1.3 %copy-start = (bf16[16,256,256]{2,1,0:T(8,128)(2,1)}, bf16[16,256,256]{2,1,0:T(8,128)(2,1)S(1)}, u32[]{:S(2)}) copy-start(bf16[16,256,256]{2,1,0:T(8,128)(2,1)S(1)} %get-tuple-element.49.mask_ref) | copy-start | bytes 6291460 | tf_op jit(solution)/shard_map/cond
  90.8 14.0 %all-to-all-start.1 = ((f32[128,1,128]{2,1,0:T(1,128)}), f32[128,1,128]{2,1,0:T(1,128)S(1)}, u32[]{:S(2)}, u32[]{:S(2)}) async-start(f32[128,1,128]{2,1,0:T(1,128)} %bitcast.3), calls=%async_computation.1 | async-start | bytes 131072 | tf_op jit(solution)/shard_map/cond/branch_0_fun/all_to_all | solution.py:464
  95.3 1.6 %copy-start.1 = (bf16[16,256,256]{2,1,0:T(8,128)(2,1)S(1)}, bf16[16,256,256]{2,1,0:T(8,128)(2,1)}, u32[]{:S(2)}) copy-start(bf16[16,256,256]{2,1,0:T(8,128)(2,1)} %copy-done) | copy-start | bytes 6291460 | tf_op jit(solution)/shard_map/cond
